TPU v7x, 256 devices: a whole 4x4x8 slice. The times are simulated.
256 devices in a mesh: layer: 8 (over z), latent: 16 (over x, y_hi, core), tok: 2 (over y_lo).
Axes of the slice: x: 4, y: 4 (y_hi: 2, y_lo: 2; y = y_hi * 2 + y_lo), z: 8, core: 2. Of those that a mesh axis runs over, the one named last changes fastest.
Arguments:
- layer_inputs: bfloat16 [8, 512, 2048], P('layer', 'tok'), may hold values from -6 to 6
- layer_targets: bfloat16 [8, 512, 2048], P('layer', ('latent', 'tok')), may hold values from -6 to 6
- encoder_weight: bfloat16 [8, 2048, 4096], P('layer', None, 'latent'), may hold values from -0.125 to 0.125
- encoder_bias: float32 [8, 4096], P('layer', 'latent'), may hold values from -1 to 1
- decoder_weight: bfloat16 [8, 4, 2, 4096, 2048], P('layer', None, 'tok', 'latent'), may hold values from -0.03125 to 0.03125
Outputs:
- reconstruction: bfloat16 [8, 512, 2048], P('layer', ('latent', 'tok'))
- encoder_grad: bfloat16 [8, 2048, 4096], P('layer', None, 'latent')
- bias_grad: float32 [8, 4096], P('layer', 'latent')
- decoder_grad: bfloat16 [8, 4, 2, 4096, 2048], P('layer', None, 'tok', 'latent')
All inputs are finite; a program needn't handle non-finite values.
Results may differ from a plain program's by a relative error of at most 0.0053.
Values may be sent and summed in bfloat16 or wider, within the bound.
A program may use at most 128 MiB of HBM per device.

v0:
```python
import jax
import jax.numpy as jnp
from jax import lax
from jax.sharding import PartitionSpec as P


def prefix(x, axis, combine, identity):
    length, index = (lax.axis_size(axis), lax.axis_index(axis))
    everything = lax.all_gather(x, axis)
    start = jnp.broadcast_to(jnp.asarray(identity, x.dtype), x.shape)

    def step(k, before):
        at = length - 1 - k
        reached = at > index
        new = combine(before, everything[at])
        return jnp.where(reached, new, before)

    return lax.fori_loop(0, length, step, start)


def smooth_gate(values):
    return jax.nn.gelu(values, approximate=True)


def shards(layer_inputs, layer_targets, encoder_weight, encoder_bias, decoder_weight):
    ways = lax.axis_size("tok")
    own_layer = lax.axis_index("layer")
    own_half = lax.axis_index("tok")
    tok_rows = layer_inputs.shape[1]
    width = layer_inputs.shape[2]
    local_latents = encoder_weight.shape[2]
    members = decoder_weight.shape[1]
    layer_count = members * ways
    all_tokens = tok_rows * ways
    preact = (
        jnp.dot(layer_inputs[0], encoder_weight[0], preferred_element_type=jnp.float32)
        + encoder_bias[0]
    )
    latents = smooth_gate(preact).astype(jnp.bfloat16)
    gathered = lax.all_gather(latents[None], ("layer", "tok"), axis=0, tiled=True)
    gathered = gathered.reshape(members, ways, ways, tok_rows, local_latents)
    sources = lax.dynamic_index_in_dim(gathered, own_half, 1, keepdims=False).reshape(
        members, all_tokens, local_latents
    )
    valid = [member * ways + own_half <= own_layer for member in range(members)]

    def decode_one(member):
        return jnp.dot(
            sources[member], decoder_weight[0, member, 0], preferred_element_type=jnp.float32
        )

    def decode_none(member):
        return jnp.zeros((all_tokens, width), jnp.float32)

    partial_sum = jnp.zeros((all_tokens, width), jnp.float32)
    for member in range(members):
        partial_sum = partial_sum + lax.cond(valid[member], decode_one, decode_none, member)
    recon = lax.psum_scatter(partial_sum, ("latent", "tok"), scatter_dimension=0, tiled=True)
    reconstruction = recon.astype(jnp.bfloat16)[None]
    error = recon - layer_targets[0].astype(jnp.float32)
    errors_all = lax.all_gather(error, ("latent", "tok"), axis=0, tiled=True)

    def weight_one(member):
        return jnp.einsum(
            "tf,td->fd",
            sources[member].astype(jnp.float32),
            errors_all,
            precision=lax.Precision.HIGHEST,
            preferred_element_type=jnp.float32,
        )

    def weight_none(member):
        return jnp.zeros((local_latents, width), jnp.float32)

    def latent_one(member):
        return jnp.einsum(
            "td,fd->tf",
            errors_all,
            decoder_weight[0, member, 0].astype(jnp.float32),
            precision=lax.Precision.HIGHEST,
            preferred_element_type=jnp.float32,
        )

    def latent_none(member):
        return jnp.zeros((all_tokens, local_latents), jnp.float32)

    weight_blocks = []
    latent_terms = []
    for member in range(members):
        weight_blocks.append(
            lax.cond(valid[member], weight_one, weight_none, member).astype(jnp.bfloat16)
        )
        latent_terms.append(lax.cond(valid[member], latent_one, latent_none, member))
    decoder_grad = jnp.stack(weight_blocks)[None, :, None]
    terms = jnp.stack(latent_terms)
    moved = lax.all_to_all(
        terms.reshape(members, 1, ways, tok_rows, local_latents),
        "tok",
        split_axis=2,
        concat_axis=1,
        tiled=True,
    )
    moved = moved.reshape(layer_count, tok_rows, local_latents)
    later = prefix(moved, "layer", jnp.add, jnp.zeros_like(moved))
    latent_grad = lax.dynamic_index_in_dim(later + moved, own_layer, 0, keepdims=False)
    unused, pullback = jax.vjp(smooth_gate, preact)
    preact_grad = pullback(latent_grad)[0]
    grad_half = preact_grad.astype(jnp.bfloat16)
    weight_sum = jnp.einsum(
        "td,tf->df", layer_inputs[0], grad_half, preferred_element_type=jnp.float32
    )
    bias_sum = jnp.sum(preact_grad, axis=0)
    weight_sum, bias_sum = lax.psum((weight_sum, bias_sum), "tok")
    encoder_grad = weight_sum.astype(jnp.bfloat16)
    return (reconstruction, encoder_grad[None], bias_sum[None], decoder_grad)


def solution(mesh):
    placed = (
        P("layer", "tok", None),
        P("layer", ("latent", "tok"), None),
        P("layer", None, "latent"),
        P("layer", "latent"),
        P("layer", None, "tok", "latent", None),
    )
    return jax.shard_map(
        shards,
        mesh=mesh,
        in_specs=placed,
        out_specs=(
            P("layer", ("latent", "tok"), None),
            P("layer", None, "latent"),
            P("layer", "latent"),
            P("layer", None, "tok", "latent", None),
        ),
        check_vma=False,
    )
```

profile of v0, /device:TPU:8, one launch (start us, length us, event | category | flops | bytes accessed | tf_op | source)
XLA Modules:
  0.0 643.1 jit_solution(15768279491832867927)
XLA Ops:
  7.2 1.2 copy-done
  8.4 2.4 multiply_convert_fusion
  10.8 0.0 reduce-scatter.2.cloned.1.call-start
  10.9 74.7 %all-gather.9.cloned.1.call-done = bf16[4096,256]{1,0:T(8,128)(2,1)} async-done(((bf16[256,256]{1,0:T(8,128)(2,1)}), bf16[4096,256]{1,0:T(8,128)(2,1)}) %all-gather.9.cloned.1.call-update) | async-done | bytes 2097168 | tf_op jit(solution)/shard_map/all_gather | solution.py:40
  85.5 1.3 constant_dynamic-slice_fusion
  86.8 2.5 conditional.13
  86.8 2.5 broadcast.46
  89.4 2.5 conditional.14
  89.4 2.5 broadcast.47
  91.9 2.5 conditional.12
  91.9 2.5 broadcast.45
  94.4 2.5 conditional.15
  94.4 2.5 broadcast.48
  96.9 10.2 %add_add_fusion = f32[512,2048]{1,0:T(8,128)} fusion(f32[512,2048]{1,0:T(8,128)} %get-tuple-element.328, f32[512,2048]{1,0:T(8,128)} %get-tuple-element.327, f32[512,2048]{1,0:T(8,128)} %get-tuple-element.325, f32[512,2048]{1,0:T(8,128)} %get-tuple-element.326), kind=kLoop, calls=%fused_computation.50 | loop fusion | flops 3145728 | bytes 20971520 | tf_op jit(solution)/shard_map/add | solution.py:57
  107.1 0.0 all-gather.5.cloned.1.call-start
  107.1 142.7 %reduce-scatter.2.cloned.1.call-done = f32[16,2048]{1,0:T(8,128)} async-done(((f32[512,2048]{1,0:T(8,128)}), f32[16,2048]{1,0:T(8,128)}) %reduce-scatter.2.cloned.1.call-update) | async-done | bytes 131088 | tf_op jit(solution)/shard_map/reduce_scatter | solution.py:58
  249.9 1.7 convert_subtract_fusion
  251.5 0.0 all-gather.7.cloned.1.call-start
  251.6 89.2 %all-gather.5.cloned.1.call-done = f32[512,2048]{1,0:T(8,128)} async-done(((f32[16,2048]{1,0:T(8,128)}), f32[512,2048]{1,0:T(8,128)}) %all-gather.5.cloned.1.call-update) | async-done | bytes 4194320 | tf_op jit(solution)/shard_map/all_gather | solution.py:61
  340.9 0.1 conditional.18
  340.9 0.2 conditional.16
  341.2 0.1 conditional.19
  341.2 0.1 pad_maximum_fusion
  341.4 31.2 %all_to_all.4 = f32[4,1,2,256,256]{4,3,1,0,2:T(8,128)S(1)} all-to-all(f32[4,1,2,256,256]{4,3,1,0,2:T(8,128)S(1)} %pad_maximum_fusion), channel_id=1, replica_groups=mesh['layer'=8,'latent'=16,'tok'=2] {'tok'}, dimensions={2} | all-to-all | bytes 4194304 | tf_op jit(solution)/shard_map/all_to_all | solution.py:96
  372.6 1.5 copy.19
  374.2 1.2 conditional.21
  374.2 1.2 stack.38
  375.4 1.1 conditional.22
  375.4 1.1 stack.40
  376.5 1.1 conditional.20
  376.5 1.1 stack.36
  377.6 1.1 conditional.23
  377.6 1.1 stack.42
  378.7 3.8 maximum_bitcast_fusion
  382.5 179.1 %all-gather.7.cloned.1.call-done = f32[8,8,256,256]{3,2,1,0:T(8,128)} async-done(((f32[1,8,256,256]{3,2,1,0:T(8,128)}), f32[8,8,256,256]{3,2,1,0:T(8,128)}) %all-gather.7.cloned.1.call-update) | async-done | bytes 16777232 | tf_op jit(solution)/shard_map/all_gather | solution.py:9
  561.6 18.7 %while.16 = (s32[]{:T(128)}, f32[8,256,256]{2,1,0:T(8,128)S(1)}, s32[]{:T(128)}, f32[8,8,256,256]{3,2,1,0:T(8,128)}, s32[]{:T(128)}, /*index=5*/s32[]{:T(128)}, s32[]{:T(128)}, s32[]{:T(128)}) while((s32[]{:T(128)}, f32[8,256,256]{2,1,0:T(8,128)S(1)}, s32[]{:T(128)}, f32[8,8,256,256]{3,2,1,0:T(8,128)}, s32[]{:T(128)}, ...), condition=%wide.region_18.19_spmd.clone, body=%wide.region_17.18_spmd.clone.sunk | while | flops 1572872 | bytes 6291611 | solution.py:18
  561.6 2.3 add_select_fusion.2
  563.9 2.3 add_select_fusion.2
  566.3 2.3 add_select_fusion.2
  568.6 2.3 add_select_fusion.2
  570.9 2.3 add_select_fusion.2
  573.3 2.3 add_select_fusion.2
  575.6 2.3 add_select_fusion.2
  577.9 2.3 add_select_fusion.2
  580.3 1.2 fusion.51
  581.4 0.5 convolution_bitcast_fusion.4
  581.9 52.4 %all-reduce.2 = (bf16[2048,256]{0,1:T(8,128)(2,1)}, f32[1,256]{1,0:T(1,128)}) all-reduce(f32[2048,256]{0,1:T(8,128)S(1)} %convolution_bitcast_fusion.4, f32[1,256]{1,0:T(1,128)S(1)} %bitcast.148), channel_id=1, replica_groups=mesh['layer'=8,'latent'=16,'tok'=2] {'tok'}, use_global_device_ids=true, to_apply=%region_19.20 | all-reduce | flops 524544 | bytes 3147776 | tf_op jit(solution)/shard_map/psum | solution.py:113
  634.3 2.3 copy.21
  (16 shorter events, 0.3 us)
Async XLA Ops:
  7.2 1.2 copy-start
  7.2 78.3 %all-gather.9.cloned.1.call-start = ((), (), s32[]{:S(2)}) async-start(), calls=%async_computation.5 | async-start | bytes 2228224 | tf_op jit(solution)/shard_map/all_gather | solution.py:40
  10.8 239.1 %reduce-scatter.2.cloned.1.call-start = ((), (), s32[]{:S(2)}) async-start(), calls=%async_computation.2 | async-start | bytes 4325376 | tf_op jit(solution)/shard_map/reduce_scatter | solution.py:58
  86.8 7.6 %copy-start.1 = (bf16[4,1,2,256,256]{4,3,2,1,0:T(8,128)(2,1)}, bf16[4,1,2,256,256]{4,3,2,1,0:T(8,128)(2,1)S(1)}, u32[]{:S(2)}) copy-start(bf16[4,1,2,256,256]{4,3,2,1,0:T(8,128)(2,1)S(1)} %constant_dynamic-slice_fusion) | copy-start | bytes 3145732
  107.1 142.8 %copy-start.2 = (bf16[1,16,2048]{2,1,0:T(8,128)(2,1)S(1)}, bf16[1,16,2048]{2,1,0:T(8,128)(2,1)}, u32[]{:S(2)}) copy-start(bf16[1,16,2048]{2,1,0:T(8,128)(2,1)} %param.32) | copy-start | bytes 196612
  107.1 233.7 %all-gather.5.cloned.1.call-start = ((), (), s32[]{:S(2)}) async-start(), calls=%async_computation.3 | async-start | bytes 4325376 | tf_op jit(solution)/shard_map/all_gather | solution.py:61
  251.5 310.0 %all-gather.7.cloned.1.call-start = ((), (), s32[]{:S(2)}) async-start(), calls=%async_computation.4 | async-start | bytes 18874368 | tf_op jit(solution)/shard_map/all_gather | solution.py:9
Sparse Core Ops, SparseCore 0:
  10.9 74.5 all-gather.8
  107.2 142.5 reduce-scatter.1
  252.2 88.5 all-gather.4
  374.3 187.2 all-gather.6
where the time goes:
time: 645 us; the launch traced here: 643 us
  waiting for transfers between devices  486 us (75%)
  blocking collectives  83.6 us (13%)
  other arithmetic  35.4 us (5%)
  local copies, waits for them, and re-layouts  21 us (3%)
  between operations  13.9 us (2%)
    all_gather x1, waiting for transfers between devices, prefix(): everything = lax.all_gather(x, axis)  179 us
    reduce_scatter x1, waiting for transfers between devices, shards(): lax.psum_scatter(partial_sum, ('latent', 'tok'), scatter_dimension=0, til...  143 us
    all_gather x1, waiting for transfers between devices, shards(): errors_all = lax.all_gather(error, ('latent', 'tok'), axis=0, tiled=True)  89.2 us
    all_gather x1, waiting for transfers between devices, shards(): lax.all_gather(latents[None], ('layer', 'tok'), axis=0, tiled=True)  74.7 us
    psum x1, blocking collectives, shards(): weight_sum, bias_sum = lax.psum((weight_sum, bias_sum), 'tok')  52.4 us
    all_to_all x1, blocking collectives, shards(): lax.all_to_all(terms.reshape(members, 1, ways, tok_rows, local_latents),...  31.2 us
    select_n x8, other arithmetic, step(): return jnp.where(reached, new, before)  18.5 us
  transfers between devices with their start and end apart: 4, of which 4 were waited for; matrix products, arithmetic and copies ran while one was open for 1% of the time, Pallas kernels for 0%

commit v1 on v0

v1 whole, which is shorter than its diff:
```python
import jax
import jax.numpy as jnp
from jax import lax
from jax.experimental import pallas as pl
from jax.experimental.pallas import tpu as pltpu
from jax.sharding import PartitionSpec as P

MESH = pl.DeviceIdType.MESH
BF = jnp.bfloat16
F32 = jnp.float32


def mul(value, by):
    return pl.multiple_of(value * by, by)


class Numbers:
    def __init__(self):
        self.count = 0

    def take(self, n=1):
        base = self.count
        self.count += n
        return base


def kernel(
    x_hbm, t_ref, we_hbm, b_ref, w_hbm,
    rec_ref, enc_hbm, bias_ref, dec_hbm,
    xp, xt, we, wp, own, latb, lt, gp, tg, p32, cs, cr, s32, ys, ra, rb, u32, xs, rx, rc, err,
    term, gr, gs, lg, pg, bs, recs, encv, dg, ss, rs, ls,
):
    z, lat, k = lax.axis_index("layer"), lax.axis_index("latent"), lax.axis_index("tok")
    x, yh, c = lat // 4, (lat // 2) % 2, lat % 2
    y = yh * 2 + k
    h = z % 2
    o = 1 - c

    def dev(dx=0, dy=0, dz=0, flip=0):
        xx, yy, zz = (x + dx) % 4, (y + dy) % 4, (z + dz) % 8
        cc = o if flip else c
        return (zz, xx * 4 + (yy // 2) * 2 + cc, yy % 2)

    mate = (z, lat, 1 - k)
    snum, rnum, lnum = Numbers(), Numbers(), Numbers()
    late = []

    def rc_(src, dst, si, ri, to):
        return pltpu.make_async_remote_copy(
            src_ref=src, dst_ref=dst, send_sem=ss.at[si], recv_sem=rs.at[ri],
            device_id=to, device_id_type=MESH,
        )

    def send(src, dst, ri, to, cond=None, si=None):
        si = snum.take() if si is None else si
        copy = rc_(src, dst, si, ri, to)
        if cond is None:
            copy.start()
        else:
            pl.when(cond)(copy.start)
        late.append((copy, cond))

    def arrived(dst, ri, cond=None):
        copy = rc_(dst, dst, 0, ri, mate)
        if cond is None:
            copy.wait_recv()
        else:
            pl.when(cond)(copy.wait_recv)

    def local(src, dst):
        copy = pltpu.make_async_copy(src, dst, ls.at[lnum.take()])
        copy.start()
        return copy

    load_x = [[local(x_hbm.at[:, :, cc, q], xp.at[q, k, cc]) for cc in range(2)] for q in range(2)]
    load_we = local(we_hbm, we)
    load_w = [
        local(
            w_hbm.at[:, hh * 1024 + ab * 512 : hh * 1024 + ab * 512 + 512],
            wp.at[:, ab * 1024 + hh * 512 : ab * 1024 + hh * 512 + 512],
        )
        for ab in range(2)
        for hh in range(2)
    ]

    barrier = pltpu.get_barrier_semaphore()
    peers = [dev(dz=1), dev(dz=-1), dev(flip=1)]
    peers += [dev(dy=d) for d in (1, 2, 3)] + [dev(dx=d) for d in (1, 2, 3)]
    for to in peers:
        pl.semaphore_signal(barrier, inc=1, device_id=to, device_id_type=MESH)

    ku = [4, 4, 3 - k, 1 - k]
    kd = [3, 3 * (1 - k), 0, 0]
    route = []
    for m in range(4):
        s = 2 * m + k
        u, d = z - s, (s - z + 8) % 8
        on_up = jnp.logical_and(u >= 1, u <= ku[m])
        on_dn = jnp.logical_and(d >= 1, d <= kd[m])
        on = jnp.logical_or(on_up, on_dn)
        dist = jnp.where(on_up, u, d)
        reach = jnp.where(on_up, ku[m], kd[m])
        passing = jnp.logical_and(on_dn, z < s)
        next_passing = jnp.logical_and(on_dn, (z + 7) % 8 < s)
        next_passing = jnp.logical_and(next_passing, z > 0)
        route.append(dict(on=on, up=on_up, dn=on_dn, dist=dist, reach=reach, passing=passing,
                          next_passing=next_passing, valid=s <= z,
                          onward=jnp.where(on_up, 1, 7), back=jnp.where(on_up, 7, 1)))
    mine = z // 2
    home = k == h
    ku_own = jnp.where(mine == 0, 4, jnp.where(mine == 1, 4, jnp.where(mine == 2, 3 - k, 1 - k)))
    kd_own = jnp.where(mine == 0, 3, jnp.where(mine == 1, 3 * (1 - k), 0))
    home_up = jnp.logical_and(home, ku_own > 0)
    home_dn = jnp.logical_and(home, kd_own > 0)
    away = jnp.logical_not(home)

    for m in range(4):
        @pl.when(jnp.logical_not(route[m]["valid"]))
        def _():
            latb[m] = jnp.zeros((512, 256), BF)

    lat_r = rnum.take(16)
    mate_x, core_x, mate_t, mate_rec, mate_bias = (rnum.take() for _ in range(5))
    pg_r = rnum.take(4)
    gr_r = rnum.take(20)

    def lat_sem(m, q, j):
        return lat_r + m * 4 + q * 2 + j

    def rows(q, j):
        kk = k if j == 0 else 1 - k
        return pl.ds(pl.multiple_of(q * 256 + kk * 128, 128), 128)

    def origin_send(q, j):
        r = rows(q, j)
        src = latb.at[mine, r]
        send(src, src, lat_sem(mine, q, j), dev(dz=1), home_up)
        slot = jnp.where(jnp.logical_and(z >= 1, z - 1 < z), 4, mine)
        send(src, latb.at[slot, r], lat_sem(mine, q, j), dev(dz=-1), home_dn)

    def gate(v):
        inner = 0.7978845608028654 * (v + 0.044715 * (v * v * v))
        t = jnp.tanh(inner)
        cdf = 0.5 * (1.0 + t)
        slope = cdf + 0.5 * v * (1.0 - t * t) * (0.7978845608028654 * (1.0 + 0.134145 * (v * v)))
        return v * cdf, slope

    def preact(q, kk):
        v = jnp.dot(xp[q, kk].reshape(128, 2048), we[...], preferred_element_type=F32) + b_ref[...]
        return gate(v)

    load_we.wait()
    for q in range(2):
        for copy in load_x[q]:
            copy.wait()
        val, slope = preact(q, k)
        val = val.astype(BF)
        own[q] = val
        gp[rows(q, 0), :] = slope

        @pl.when(home)
        def _():
            latb[mine, rows(q, 0), :] = val

        if q == 0:
            pl.semaphore_wait(barrier, len(peers))
        send(own.at[q], latb.at[mine, rows(q, 0)], lat_sem(mine, q, 1), mate, away)
        origin_send(q, 0)

    tg[k] = t_ref[:, pl.ds(mul(k, 1024), 1024)]
    send(t_ref.at[:, pl.ds(mul(1 - k, 1024), 1024)], tg.at[k], mate_t, mate)
    send(xp.at[c, k], xp.at[c, k], mate_x, mate)

    def lat_relay(q):
        for j in range(2):
            if j == 1:
                arrived(latb.at[mine, rows(q, 1)], lat_sem(mine, q, 1), home)
                origin_send(q, 1)
        for far in (1, 2, 3):
            for j in range(2):
                for m in range(3):
                    if far == 3 and m == 2:
                        continue
                    e = route[m]
                    cond = jnp.logical_and(e["on"], jnp.logical_and(e["dist"] == far, e["dist"] < e["reach"]))
                    src = latb.at[jnp.where(e["passing"], 4, m), rows(q, j)]
                    dst = latb.at[jnp.where(e["next_passing"], 4, m), rows(q, j)]
                    arrived(src, lat_sem(m, q, j), cond)
                    send(src, dst, lat_sem(m, q, j), dev(dz=e["onward"]), cond)

    def lat_last(q):
        for j in range(2):
            for m in range(4):
                e = route[m]
                cond = jnp.logical_and(e["on"], e["dist"] == e["reach"])
                arrived(latb.at[m, rows(q, j)], lat_sem(m, q, j), cond)

    piece = {}
    for q in range(2):
        for ab in range(2):
            piece[q, ab] = dict(core=rnum.take(), a=rnum.take(3), b=rnum.take(3), g1=rnum.take(3),
                                g2=rnum.take(3), g3=rnum.take())

    def decode(q):
        for ab in range(2):
            def tile(i, _):
                left = jnp.concatenate([latb[m, q * 256 : q * 256 + 256, :] for m in range(4)], axis=1)
                at = pl.multiple_of(ab * 1024 + i * 256, 256)
                part = jnp.dot(left, wp[:, pl.ds(at, 256)], preferred_element_type=F32)
                p32[ab, :, :, :, pl.ds(mul(i, 256), 256)] = part.reshape(2, 2, 64, 256)
                return 0

            lax.fori_loop(0, 4, tile, 0)
            cs[q, ab] = p32[ab, :, o].astype(BF)
            send(cs.at[q, ab], cr.at[q, ab], piece[q, ab]["core"], dev(flip=1))

    def stage_a(q):
        for ab in range(2):
            arrived(cr.at[q, ab], piece[q, ab]["core"])
            total = (p32[ab, :, c] + cr[q, ab].astype(F32)).reshape(4, 2, 16, 1024)
            s32[ab] = total
            ys[q, ab] = total.astype(BF)
            for d in (1, 2, 3):
                sem = piece[q, ab]["a"] + d - 1
                if ab == 0:
                    to = (y + d) % 4
                    src = ys.at[q, 0, :, to // 2, :, pl.ds(mul(to % 2, 512), 512)]
                    send(src, ra.at[q, d - 1], sem, dev(dy=d))
                else:
                    send(ys.at[q, 1, (x + d) % 4], rb.at[q, d - 1], sem, dev(dx=d))

    def stage_b(q):
        for ab in range(2):
            buf = ra if ab == 0 else rb
            for d in (1, 2, 3):
                arrived(buf.at[q, d - 1], piece[q, ab]["a"] + d - 1)
            if ab == 0:
                total = s32[0, :, yh, :, pl.ds(mul(k, 512), 512)]
            else:
                total = s32[1, x]
            for d in range(3):
                total = total + buf[q, d].astype(F32)
            if ab == 0:
                u32[0] = total
                xs[q, 0] = total.astype(BF)
            else:
                for yy in range(4):
                    block = total[yy // 2, :, (yy % 2) * 512 : (yy % 2) * 512 + 512]
                    u32[1, yy] = block
                    xs[q, 1, yy] = block.astype(BF)
            for d in (1, 2, 3):
                sem = piece[q, ab]["b"] + d - 1
                if ab == 0:
                    send(xs.at[q, 0, (x + d) % 4], rx.at[q, 0, d - 1], sem, dev(dx=d))
                else:
                    send(xs.at[q, 1, (y + d) % 4], rx.at[q, 1, d - 1], sem, dev(dy=d))

    def block_of(q, ab, xx, yy):
        cols = pl.ds(pl.multiple_of(ab * 1024 + (yy % 2) * 512, 512), 512)
        return err.at[q, xx // 2, c, xx % 2, yy // 2, :, cols]

    def line_of(q, ab, xx, yy):
        if ab == 0:
            cols = pl.ds(mul(yy % 2, 512), 512)
            return err.at[q, :, c, :, yy // 2, :, cols]
        return err.at[q, xx // 2, c, xx % 2, :, :, 1024:2048]

    def stage_c(q):
        for ab in range(2):
            for d in (1, 2, 3):
                arrived(rx.at[q, ab, d - 1], piece[q, ab]["b"] + d - 1)
            total = u32[ab, x if ab == 0 else y]
            for d in range(3):
                total = total + rx[q, ab, d].astype(F32)
            rc[q, :, ab * 512 : ab * 512 + 512] = total.astype(BF)
            diff = total - tg[q, :, ab * 512 : ab * 512 + 512].astype(F32)
            cols = pl.ds(pl.multiple_of(ab * 1024 + k * 512, 512), 512)
            err[q, x // 2, c, x % 2, yh, :, cols] = diff.astype(BF)
            mine_ = block_of(q, ab, x, y)
            for d in (1, 2, 3):
                to = dev(dx=d) if ab == 0 else dev(dy=d)
                send(mine_, mine_, piece[q, ab]["g1"] + d - 1, to)

    def stage_d(q):
        for ab in range(2):
            for d in (1, 2, 3):
                if ab == 0:
                    block = block_of(q, 0, (x - d + 4) % 4, y)
                else:
                    block = block_of(q, 1, x, (y - d + 4) % 4)
                arrived(block, piece[q, ab]["g1"] + d - 1)
            line = line_of(q, ab, x, y)
            for d in (1, 2, 3):
                to = dev(dy=d) if ab == 0 else dev(dx=d)
                send(line, line, piece[q, ab]["g2"] + d - 1, to)

    def stage_e(q):
        for ab in range(2):
            for d in (1, 2, 3):
                line = line_of(q, ab, (x - d + 4) % 4, (y - d + 4) % 4)
                arrived(line, piece[q, ab]["g2"] + d - 1)
            half = err.at[q, :, c, :, :, :, ab * 1024 : ab * 1024 + 1024]
            send(half, half, piece[q, ab]["g3"], dev(flip=1))

    def stage_f(q):
        for ab in range(2):
            arrived(err.at[q, :, o, :, :, :, ab * 1024 : ab * 1024 + 1024], piece[q, ab]["g3"])

        def one(m, _):
            term[q, m] = lax.dot_general(
                err[q].reshape(256, 2048), wp[pl.ds(mul(m, 256), 256), :],
                (((1,), (1,)), ((), ())), preferred_element_type=F32,
            )
            return 0

        lax.fori_loop(0, 4, one, 0)

    def grad_step(q, depth):
        for j in range(2):
            for m in range(4):
                if depth > (3, 3, 2, 0)[m]:
                    continue
                e = route[m]
                cond = jnp.logical_and(e["on"], e["reach"] - e["dist"] == depth)
                sem = gr_r + m * 4 + q * 2 + j
                r = slice(q * 256 + j * 128, q * 256 + j * 128 + 128)
                tr = slice(j * 128, j * 128 + 128)
                if depth:
                    arrived(gr.at[m, r], sem, cond)

                @pl.when(cond)
                def _():
                    part = term[q, m, tr, :]
                    if depth:
                        part = jnp.where(e["passing"], 0.0, part) + gr[m, r, :].astype(F32)
                    gs[m, r, :] = part.astype(BF)

                last = jnp.logical_and(e["dn"], e["dist"] == 1)
                slot = jnp.where(last, 4, m)
                send(gs.at[m, r], gr.at[slot, r], gr_r + slot * 4 + q * 2 + j, dev(dz=e["back"]), cond)

    def finish(q, j):
        r = slice(q * 256 + j * 128, q * 256 + j * 128 + 128)
        tr = slice(j * 128, j * 128 + 128)
        i = q * 2 + j

        @pl.when(home)
        def _():
            lg[...] = term[q, mine, tr, :]

        arrived(gr.at[mine, r], gr_r + mine * 4 + i, home_up)

        @pl.when(home_up)
        def _():
            lg[...] += gr[mine, r, :].astype(F32)

        arrived(gr.at[4, r], gr_r + 16 + i, home_dn)

        @pl.when(home_dn)
        def _():
            lg[...] += gr[4, r, :].astype(F32)

        @pl.when(home)
        def _():
            grad = lg[...] * gp[r, :]
            pg[r, :] = grad.astype(BF)
            total = jnp.sum(grad, axis=0, keepdims=True)
            if i == 0:
                bs[...] = jnp.broadcast_to(total, (8, 256))
            else:
                bs[...] += jnp.broadcast_to(total, (8, 256))

        send(pg.at[r], pg.at[r], pg_r + i, mate, home)

    def flip_inputs(q, kk):
        def one(i, _):
            block = xp[q, kk, :, :, :, :, pl.ds(mul(i, 256), 256)].reshape(128, 256)
            xt[pl.ds(mul(i, 256), 256), q * 256 + kk * 128 : q * 256 + kk * 128 + 128] = block.T
            return 0

        lax.fori_loop(0, 8, one, 0)

    def flip_latents(q):
        for m in range(4):
            lt[m * 256 : m * 256 + 256, q * 256 : q * 256 + 256] = latb[m, q * 256 : q * 256 + 256, :].T

    dec_copies = {}

    def dec_part(i):
        ab, hh = i // 2, i % 2
        if i >= 2:
            dec_copies[i - 2].wait()

        def tile(t, _):
            at = pl.multiple_of(i * 512 + t * 256, 256)
            right = err[:, :, :, :, :, :, pl.ds(at, 256)].reshape(512, 256)
            out = jnp.dot(lt[...], right, preferred_element_type=F32)
            dg[i % 2, :, pl.ds(mul(t, 256), 256)] = out.astype(BF)
            return 0

        lax.fori_loop(0, 2, tile, 0)
        start = hh * 1024 + ab * 512
        dec_copies[i] = local(dg.at[i % 2], dec_hbm.at[:, start : start + 512])

    lat_relay(0)
    lat_last(0)
    for copy in load_w:
        copy.wait()
    decode(0)
    stage_a(0)
    lat_relay(1)
    flip_latents(0)
    stage_b(0)
    lat_last(1)
    decode(1)
    arrived(tg.at[1 - k], mate_t)
    stage_c(0)
    stage_a(1)
    stage_d(0)
    arrived(xp.at[c, 1 - k], mate_x)
    send(xp.at[c, 1 - k], xp.at[c, 1 - k], core_x, dev(flip=1))
    flip_latents(1)
    stage_b(1)
    stage_e(0)
    stage_c(1)
    arrived(xp.at[o, 1 - k], core_x)
    for q in range(2):
        gp[rows(q, 1), :] = preact(q, 1 - k)[1]
    stage_f(0)
    grad_step(0, 0)
    stage_d(1)
    flip_inputs(0, 0)
    flip_inputs(0, 1)
    stage_e(1)
    grad_step(0, 1)
    flip_inputs(1, 0)
    flip_inputs(1, 1)
    stage_f(1)
    grad_step(1, 0)
    recs[:, pl.ds(mul(k, 1024), 1024)] = rc[k]
    send(rc.at[1 - k], recs.at[:, pl.ds(mul(k, 1024), 1024)], mate_rec, mate)
    grad_step(0, 2)
    dec_part(0)
    grad_step(1, 1)
    grad_step(0, 3)
    dec_part(1)
    grad_step(1, 2)
    dec_part(2)
    finish(0, 0)
    finish(0, 1)
    grad_step(1, 3)
    dec_part(3)
    finish(1, 0)
    finish(1, 1)
    send(bs, bs, mate_bias, mate, home)
    for i in range(4):
        r = slice(i * 128, i * 128 + 128)
        arrived(pg.at[r], pg_r + i, away)

    def enc_tile(i, _):
        r = pl.ds(mul(i, 256), 256)
        encv[r, :] = jnp.dot(xt[r, :], pg[...], preferred_element_type=F32).astype(BF)
        return 0

    lax.fori_loop(0, 8, enc_tile, 0)
    enc_copy = local(encv, enc_hbm)
    arrived(bs, mate_bias, away)
    bias_ref[...] = bs[0:1, :]
    arrived(recs.at[:, pl.ds(mul(1 - k, 1024), 1024)], mate_rec)
    rec_ref[...] = recs[...]
    for copy, cond in late:
        if cond is None:
            copy.wait_send()
        else:
            pl.when(cond)(copy.wait_send)
    dec_copies[2].wait()
    dec_copies[3].wait()
    enc_copy.wait()
    assert snum.count <= 200 and rnum.count <= 120 and lnum.count <= 20, (snum.count, rnum.count)


def shards(layer_inputs, layer_targets, encoder_weight, encoder_bias, decoder_weight):
    vm, hbm = pl.BlockSpec(memory_space=pltpu.VMEM), pl.BlockSpec(memory_space=pl.ANY)
    scratch = [
        pltpu.VMEM((2, 2, 2, 2, 2, 16, 2048), BF),
        pltpu.VMEM((2048, 512), BF),
        pltpu.VMEM((2048, 256), BF),
        pltpu.VMEM((1024, 2048), BF),
        pltpu.VMEM((2, 128, 256), BF),
        pltpu.VMEM((5, 512, 256), BF),
        pltpu.VMEM((1024, 512), BF),
        pltpu.VMEM((512, 256), F32),
        pltpu.VMEM((2, 16, 1024), BF),
        pltpu.VMEM((2, 2, 2, 64, 1024), F32),
        pltpu.VMEM((2, 2, 2, 64, 1024), BF),
        pltpu.VMEM((2, 2, 2, 64, 1024), BF),
        pltpu.VMEM((2, 4, 2, 16, 1024), F32),
        pltpu.VMEM((2, 2, 4, 2, 16, 1024), BF),
        pltpu.VMEM((2, 3, 4, 16, 512), BF),
        pltpu.VMEM((2, 3, 2, 16, 1024), BF),
        pltpu.VMEM((2, 4, 16, 512), F32),
        pltpu.VMEM((2, 2, 4, 16, 512), BF),
        pltpu.VMEM((2, 2, 3, 16, 512), BF),
        pltpu.VMEM((2, 16, 1024), BF),
        pltpu.VMEM((2, 2, 2, 2, 2, 16, 2048), BF),
        pltpu.VMEM((2, 4, 256, 256), F32),
        pltpu.VMEM((5, 512, 256), BF),
        pltpu.VMEM((4, 512, 256), BF),
        pltpu.VMEM((128, 256), F32),
        pltpu.VMEM((512, 256), BF),
        pltpu.VMEM((8, 256), F32),
        pltpu.VMEM((16, 2048), BF),
        pltpu.VMEM((2048, 256), BF),
        pltpu.VMEM((2, 1024, 512), BF),
        pltpu.SemaphoreType.DMA((200,)),
        pltpu.SemaphoreType.DMA((120,)),
        pltpu.SemaphoreType.DMA((20,)),
    ]
    rec, enc, bias, dec = pl.pallas_call(
        kernel,
        out_shape=(
            jax.ShapeDtypeStruct((16, 2048), BF),
            jax.ShapeDtypeStruct((2048, 256), BF),
            jax.ShapeDtypeStruct((1, 256), F32),
            jax.ShapeDtypeStruct((1024, 2048), BF),
        ),
        in_specs=[hbm, vm, hbm, vm, hbm],
        out_specs=(vm, hbm, vm, hbm),
        scratch_shapes=scratch,
        compiler_params=pltpu.CompilerParams(
            collective_id=0, has_side_effects=True, vmem_limit_bytes=56 * 1024 * 1024
        ),
        name="transcoder_step",
    )(
        layer_inputs.reshape(2, 2, 2, 2, 16, 2048),
        layer_targets[0],
        encoder_weight[0],
        encoder_bias,
        decoder_weight.reshape(1024, 2048),
    )
    return rec[None], enc[None], bias, dec.reshape(1, 4, 1, 256, 2048)


def solution(mesh):
    placed = (
        P("layer", "tok", None),
        P("layer", ("latent", "tok"), None),
        P("layer", None, "latent"),
        P("layer", "latent"),
        P("layer", None, "tok", "latent", None),
    )
    return jax.shard_map(
        shards,
        mesh=mesh,
        in_specs=placed,
        out_specs=(
            P("layer", ("latent", "tok"), None),
            P("layer", None, "latent"),
            P("layer", "latent"),
            P("layer", None, "tok", "latent", None),
        ),
        check_vma=False,
    )
```

time: 645 us -> 99.7 us (0.15)
  waiting for transfers between devices: 486 us -> 0 us
  Pallas kernels: 0 us -> 89.1 us
  blocking collectives: 83.6 us -> 0 us
  other arithmetic: 35.4 us -> 0 us
  between operations: 13.9 us -> 0.64 us
  local copies, waits for them, and re-layouts: 21 us -> 9.74 us
    all_gather x3 -> x0, waiting for transfers between devices: 343 us -> none  [the longest x1 179 us: prefix(): everything = lax.all_gather(x, axis)]
    reduce_scatter x1 -> x0, waiting for transfers between devices: 143 us -> none  [shards(): lax.psum_scatter(partial_sum, ('latent', 'tok'), scatter_dimension=0, til...]
    pallas_call x0 -> x1, Pallas kernels: none -> 89.1 us  [shards(): pl.pallas_call(kernel, out_shape=(jax.ShapeDtypeStruct((16, 2048), BF), j...]
    psum x1 -> x0, blocking collectives: 52.4 us -> none  [shards(): weight_sum, bias_sum = lax.psum((weight_sum, bias_sum), 'tok')]
    all_to_all x1 -> x0, blocking collectives: 31.2 us -> none  [shards(): lax.all_to_all(terms.reshape(members, 1, ways, tok_rows, local_latents),...]
    select_n x8 -> x0, other arithmetic: 18.5 us -> none  [step(): return jnp.where(reached, new, before)]
    another operation x12 -> x0, local copies, waits for them, and re-layouts: 14.7 us -> none
    add x1 -> x0, other arithmetic: 10.2 us -> none  [shards(): partial_sum + lax.cond(valid[member], decode_one, decode_none, member)]
  transfers between devices with their start and end apart: 4 -> 0, of which waited for: 4 -> 0; matrix products, arithmetic and copies ran while one was open for 1% -> 0% of each run, Pallas kernels for 0% -> 0%
where the time goes in v1:
time: 99.7 us; the launch traced here: 99.4 us
  Pallas kernels  89.1 us (89%)
  local copies, waits for them, and re-layouts  9.74 us (10%)
    pallas_call x1, Pallas kernels, shards(): pl.pallas_call(kernel, out_shape=(jax.ShapeDtypeStruct((16, 2048), BF), j...  89.1 us
    unnamed x4, local copies, waits for them, and re-layouts  9.74 us

profile of v1, /device:TPU:8, one launch (start us, length us, event | category | flops | bytes accessed | tf_op | source)
XLA Modules:
  0.0 99.4 jit_solution(10721897710434960000)
XLA Ops:
  0.6 89.1 %transcoder_step.1 = (bf16[16,2048]{1,0:T(8,128)(2,1)}, bf16[2048,256]{1,0:T(8,128)(2,1)}, f32[1,256]{1,0:T(1,128)}, bf16[1024,2048]{1,0:T(8,128)(2,1)}) custom-call(bf16[2,2,2,2,16,2048]{5,4,3,2,1,0:T(8,128)(2,1)} %bitcast.12, bf16[16,2048]{1,0:T(8,128)(2,1)} %bitcast.14, bf16[2048,256]{1,0:T(8,128)(2,1)} %bitcast.13, f32[1,256]{1,0:T(1,128)} %b_ref.1, ...), custom_call_target="tpu_custom_call" | custom-call | tf_op jit(solution)/shard_map/transcoder_step/pallas_call | solution.py:519
  89.7 1.5 %copy.14 = bf16[1,16,2048]{2,1,0:T(8,128)(2,1)} copy(bf16[1,16,2048]{2,1,0:T(8,128)(2,1)} %bitcast.15) | data formatting | bytes 131072
  91.2 2.3 %copy.15 = bf16[1,2048,256]{2,1,0:T(8,128)(2,1)} copy(bf16[1,2048,256]{2,1,0:T(8,128)(2,1)} %bitcast.11) | data formatting | bytes 2097152
  93.4 1.2 %copy.16 = f32[1,256]{1,0:T(1,128)} copy(f32[1,256]{1,0:T(1,128)} %get-tuple-element.22) | data formatting | bytes 2048
  94.7 4.8 %copy.17 = bf16[1,4,1,256,2048]{4,3,2,1,0:T(8,128)(2,1)} copy(bf16[1,4,1,256,2048]{4,3,2,1,0:T(8,128)(2,1)} %bitcast.10) | data formatting | bytes 8388608

commit v2 on v1

v2 whole, which is shorter than its diff:
```python
import jax
import jax.numpy as jnp
from jax import lax
from jax.experimental import pallas as pl
from jax.experimental.pallas import tpu as pltpu
from jax.sharding import PartitionSpec as P

MESH = pl.DeviceIdType.MESH
SPLIT = 2
SUB = 128 // SPLIT
COUNTS = (47, 109, 12)
BF = jnp.bfloat16
F32 = jnp.float32


def mul(value, by):
    return pl.multiple_of(value * by, by)


class Numbers:
    def __init__(self):
        self.count = 0

    def take(self, n=1):
        base = self.count
        self.count += n
        return base


def kernel(
    x_hbm, t_hbm, we_hbm, b_hbm, w_hbm,
    rec_hbm, bias_hbm, pg_hbm, xt_hbm, dec_hbm,
    t_ref, b_ref,    xp, xt, we, wp, own, latb, lt, gp, tg, p32, cs, cr, s32, ys, ra, rb, u32, xs, rx, rc, err,
    term, gr, gs, lg, pg, bs, recs, dg, ss, rs, ls,
):
    z, lat, k = lax.axis_index("layer"), lax.axis_index("latent"), lax.axis_index("tok")
    x, yh, c = lat // 4, (lat // 2) % 2, lat % 2
    y = yh * 2 + k
    h = z % 2
    o = 1 - c

    def dev(dx=0, dy=0, dz=0, flip=0):
        xx, yy, zz = (x + dx) % 4, (y + dy) % 4, (z + dz) % 8
        cc = o if flip else c
        return (zz, xx * 4 + (yy // 2) * 2 + cc, yy % 2)

    mate = (z, lat, 1 - k)
    snum, rnum, lnum = Numbers(), Numbers(), Numbers()
    sent = []

    def rc_(src, dst, si, ri, to):
        return pltpu.make_async_remote_copy(
            src_ref=src, dst_ref=dst, send_sem=ss.at[si], recv_sem=rs.at[ri],
            device_id=to, device_id_type=MESH,
        )

    def group(like, cond=None):
        si = snum.take()
        sent.append((si, like, cond))
        return si

    def send(src, dst, si, ri, to, cond=None):
        copy = rc_(src, dst, si, ri, to)
        if cond is None:
            copy.start()
        else:
            pl.when(cond)(copy.start)

    def arrived(dst, ri, cond=None):
        copy = rc_(dst, dst, 0, ri, mate)
        if cond is None:
            copy.wait_recv()
        else:
            pl.when(cond)(copy.wait_recv)

    def local(src, dst, li=None):
        copy = pltpu.make_async_copy(src, dst, ls.at[lnum.take() if li is None else li])
        copy.start()
        return copy

    def landed(dst, li):
        pltpu.make_async_copy(dst, dst, ls.at[li]).wait()

    load_x = [lnum.take(), lnum.take()]
    for cc in range(2):
        local(x_hbm.at[:, :, cc, 0], xp.at[0, k, cc], load_x[0])
    load_we = local(we_hbm, we)
    load_b = local(b_hbm, b_ref)
    for cc in range(2):
        local(x_hbm.at[:, :, cc, 1], xp.at[1, k, cc], load_x[1])

    load_t = local(t_hbm, t_ref)

    barrier = pltpu.get_barrier_semaphore()
    peers = [dev(dz=1), dev(dz=-1), dev(flip=1)]
    peers += [dev(dy=d) for d in (1, 2, 3)] + [dev(dx=d) for d in (1, 2, 3)]
    for to in peers:
        pl.semaphore_signal(barrier, inc=1, device_id=to, device_id_type=MESH)

    ku = [4, 4, 3 - k, 1 - k]
    kd = [3, 3 * (1 - k), 0, 0]
    route = []
    for m in range(4):
        s = 2 * m + k
        u, d = z - s, (s - z + 8) % 8
        on_up = jnp.logical_and(u >= 1, u <= ku[m])
        on_dn = jnp.logical_and(d >= 1, d <= kd[m])
        on = jnp.logical_or(on_up, on_dn)
        dist = jnp.where(on_up, u, d)
        reach = jnp.where(on_up, ku[m], kd[m])
        passing = jnp.logical_and(on_dn, z < s)
        next_passing = jnp.logical_and(on_dn, (z + 7) % 8 < s)
        next_passing = jnp.logical_and(next_passing, z > 0)
        route.append(dict(on=on, up=on_up, dn=on_dn, dist=dist, reach=reach, passing=passing,
                          next_passing=next_passing, valid=s <= z,
                          onward=jnp.where(on_up, 1, 7), back=jnp.where(on_up, 7, 1)))
    mine = z // 2
    home = k == h
    ku_own = jnp.where(mine == 0, 4, jnp.where(mine == 1, 4, jnp.where(mine == 2, 3 - k, 1 - k)))
    kd_own = jnp.where(mine == 0, 3, jnp.where(mine == 1, 3 * (1 - k), 0))
    home_up = jnp.logical_and(home, ku_own > 0)
    home_dn = jnp.logical_and(home, kd_own > 0)
    away = jnp.logical_not(home)

    def clear():
        for m in range(4):
            @pl.when(jnp.logical_not(route[m]["valid"]))
            def _():
                latb[m] = jnp.zeros((512, 256), BF)

    lat_r = rnum.take(16 * SPLIT)
    mate_x, core_x, mate_t, mate_rec, mate_bias = (rnum.take() for _ in range(5))
    pg_r = rnum.take(4 * SPLIT)
    gr_r = rnum.take(20 * SPLIT)

    def lat_sem(m, q, j):
        return lat_r + m * (4 * SPLIT) + q * (2 * SPLIT) + j

    def rows(q, j):
        kk = k if j == 0 else 1 - k
        return pl.ds(pl.multiple_of(q * 256 + kk * 128, 128), 128)

    def some(q, j):
        kk = k if j < SPLIT else 1 - k
        return pl.ds(pl.multiple_of(q * 256 + kk * 128 + (j % SPLIT) * SUB, SUB), SUB)

    up_si, dn_si = group(latb.at[0], home_up), group(latb.at[0], home_dn)
    away_si, pg_si = group(own, away), group(pg, home)
    lat_si = [[snum.take() for m in range(3)] for q in range(2)]
    gr_si = [[snum.take() for m in range(4)] for q in range(2)]

    def origin_send(q, j):
        r = some(q, j)
        src = latb.at[mine, r]
        send(src, src, up_si, lat_sem(mine, q, j), dev(dz=1), home_up)
        slot = jnp.where(z >= 1, 4, mine)
        send(src, latb.at[slot, r], dn_si, lat_sem(mine, q, j), dev(dz=-1), home_dn)

    def gate(v):
        inner = 0.7978845608028654 * (v + 0.044715 * (v * v * v))
        t = jnp.tanh(inner)
        cdf = 0.5 * (1.0 + t)
        slope = cdf + 0.5 * v * (1.0 - t * t) * (0.7978845608028654 * (1.0 + 0.134145 * (v * v)))
        return v * cdf, slope

    def preact(q, kk):
        v = jnp.dot(xp[q, kk].reshape(128, 2048), we[...], preferred_element_type=F32) + b_ref[...]
        return gate(v)

    def encode(q):
        landed(xp.at[q, k], load_x[q])
        val, slope = preact(q, k)
        val = val.astype(BF)
        own[q] = val
        gp[rows(q, 0), :] = slope

        @pl.when(home)
        def _():
            latb[mine, rows(q, 0), :] = val

    def first_send(q):
        for j in range(SPLIT):
            src = own.at[q, j * SUB : j * SUB + SUB]
            send(src, latb.at[mine, some(q, j)], away_si, lat_sem(mine, q, SPLIT + j), mate, away)
            origin_send(q, j)

    def send_inputs():
        load_t.wait()
        tg[k] = t_ref[:, pl.ds(mul(k, 1024), 1024)]
        send(t_ref.at[:, pl.ds(mul(1 - k, 1024), 1024)], tg.at[k], group(tg.at[k]), mate_t, mate)
        send(xp.at[c, k], xp.at[c, k], group(xp.at[c, k]), mate_x, mate)

    def lat_hop(q, far):
        if far == 0:
            for j in range(SPLIT, 2 * SPLIT):
                arrived(latb.at[mine, some(q, j)], lat_sem(mine, q, j), home)
                origin_send(q, j)
            return
        conds = []
        for m in range(3):
            e = route[m]
            cond = jnp.logical_and(e["on"], jnp.logical_and(e["dist"] == far, e["dist"] < e["reach"]))
            conds.append(cond)
            if not (far == 3 and m == 2):
                sent.append((lat_si[q][m], latb.at[0, 0:256], cond))
        for kk in range(2):
            for m in range(3):
                if far == 3 and m == 2:
                    continue
                e = route[m]

                @pl.when(conds[m])
                def _():
                    for j in range(kk * SPLIT, kk * SPLIT + SPLIT):
                        src = latb.at[jnp.where(e["passing"], 4, m), some(q, j)]
                        dst = latb.at[jnp.where(e["next_passing"], 4, m), some(q, j)]
                        arrived(src, lat_sem(m, q, j))
                        send(src, dst, lat_si[q][m], lat_sem(m, q, j), dev(dz=e["onward"]))

    def lat_last(q):
        for m in range(4):
            e = route[m]

            @pl.when(jnp.logical_and(e["on"], e["dist"] == e["reach"]))
            def _():
                for j in range(2 * SPLIT):
                    arrived(latb.at[m, some(q, j)], lat_sem(m, q, j))

    piece = {}
    for q in range(2):
        for ab in range(2):
            piece[q, ab] = {name: rnum.take() for name in ("core", "a", "b", "g1", "g2", "g3")}

    def decode(q, ab):
        left = jnp.concatenate([latb[m, q * 256 : q * 256 + 256, :] for m in range(4)], axis=1)
        part = jnp.dot(left, wp[:, ab * 1024 : ab * 1024 + 1024], preferred_element_type=F32)
        p32[ab] = part.reshape(2, 2, 64, 1024)
        cs[q, ab] = p32[ab, :, o].astype(BF)
        send(cs.at[q, ab], cr.at[q, ab], group(cs.at[q, ab]), piece[q, ab]["core"], dev(flip=1))

    def stage_a(q):
        for ab in range(2):
            arrived(cr.at[q, ab], piece[q, ab]["core"])
            total = (p32[ab, :, c] + cr[q, ab].astype(F32)).reshape(4, 2, 16, 1024)
            s32[ab] = total
            ys[q, ab] = total.astype(BF)
            wide = ra.at[q] if ab == 0 else rb.at[q]
            si, sem = group(wide), piece[q, ab]["a"]
            for d in (1, 2, 3):
                if ab == 0:
                    to = (y + d) % 4
                    src = ys.at[q, 0, :, to // 2, :, pl.ds(mul(to % 2, 512), 512)]
                    send(src, ra.at[q, d - 1], si, sem, dev(dy=d))
                else:
                    send(ys.at[q, 1, (x + d) % 4], rb.at[q, d - 1], si, sem, dev(dx=d))

    def stage_b(q):
        for ab in range(2):
            buf = ra if ab == 0 else rb
            arrived(buf.at[q], piece[q, ab]["a"])
            if ab == 0:
                total = s32[0, :, yh, :, pl.ds(mul(k, 512), 512)]
            else:
                total = s32[1, x]
            for d in range(3):
                total = total + buf[q, d].astype(F32)
            if ab == 0:
                u32[0] = total
                xs[q, 0] = total.astype(BF)
            else:
                for yy in range(4):
                    block = total[yy // 2, :, (yy % 2) * 512 : (yy % 2) * 512 + 512]
                    u32[1, yy] = block
                    xs[q, 1, yy] = block.astype(BF)
            si, sem = group(rx.at[q, ab]), piece[q, ab]["b"]
            for d in (1, 2, 3):
                if ab == 0:
                    send(xs.at[q, 0, (x + d) % 4], rx.at[q, 0, d - 1], si, sem, dev(dx=d))
                else:
                    send(xs.at[q, 1, (y + d) % 4], rx.at[q, 1, d - 1], si, sem, dev(dy=d))

    def block_of(q, ab, xx, yy):
        cols = pl.ds(pl.multiple_of(ab * 1024 + (yy % 2) * 512, 512), 512)
        return err.at[q, xx // 2, c, xx % 2, yy // 2, :, cols]

    def line_of(q, ab, xx, yy):
        if ab == 0:
            cols = pl.ds(mul(yy % 2, 512), 512)
            return err.at[q, :, c, :, yy // 2, :, cols]
        return err.at[q, xx // 2, c, xx % 2, :, :, 1024:2048]

    def stage_c(q):
        for ab in range(2):
            arrived(rx.at[q, ab], piece[q, ab]["b"])
            total = u32[ab, x if ab == 0 else y]
            for d in range(3):
                total = total + rx[q, ab, d].astype(F32)
            rc[q, :, ab * 512 : ab * 512 + 512] = total.astype(BF)
            diff = total - tg[q, :, ab * 512 : ab * 512 + 512].astype(F32)
            cols = pl.ds(pl.multiple_of(ab * 1024 + k * 512, 512), 512)
            err[q, x // 2, c, x % 2, yh, :, cols] = diff.astype(BF)
            mine_ = block_of(q, ab, x, y)
            si = group(rx.at[q, ab])
            for d in (1, 2, 3):
                to = dev(dx=d) if ab == 0 else dev(dy=d)
                send(mine_, mine_, si, piece[q, ab]["g1"], to)

    def stage_d(q):
        for ab in range(2):
            arrived(rx.at[q, ab], piece[q, ab]["g1"])
            line = line_of(q, ab, x, y)
            si = group(ra.at[q])
            for d in (1, 2, 3):
                to = dev(dy=d) if ab == 0 else dev(dx=d)
                send(line, line, si, piece[q, ab]["g2"], to)

    def stage_e(q):
        for ab in range(2):
            arrived(ra.at[q], piece[q, ab]["g2"])
            half = err.at[q, :, c, :, :, :, ab * 1024 : ab * 1024 + 1024]
            send(half, half, group(half), piece[q, ab]["g3"], dev(flip=1))

    def stage_f(q):
        for ab in range(2):
            arrived(err.at[q, :, o, :, :, :, ab * 1024 : ab * 1024 + 1024], piece[q, ab]["g3"])

        for half in range(2):
            out = lax.dot_general(
                err[q].reshape(256, 2048), wp[half * 512 : half * 512 + 512, :],
                (((1,), (1,)), ((), ())), preferred_element_type=F32,
            )
            term[q, 2 * half] = out[:, :256]
            term[q, 2 * half + 1] = out[:, 256:]

    def grad_step(q, depth):
        for m in range(4):
            if depth > (3, 3, 2, 0)[m]:
                continue
            e = route[m]
            cond = jnp.logical_and(e["on"], e["reach"] - e["dist"] == depth)
            sent.append((gr_si[q][m], latb.at[0, 0:256], cond))

            @pl.when(cond)
            def _():
                slot = jnp.where(jnp.logical_and(e["dn"], e["dist"] == 1), 4, m)
                for j in range(2 * SPLIT):
                    sem = gr_r + m * (4 * SPLIT) + q * (2 * SPLIT) + j
                    r = slice(q * 256 + j * SUB, q * 256 + j * SUB + SUB)
                    part = term[q, m, j * SUB : j * SUB + SUB, :]
                    if depth:
                        arrived(gr.at[m, r], sem)
                        part = jnp.where(e["passing"], 0.0, part) + gr[m, r, :].astype(F32)
                    gs[m, r, :] = part.astype(BF)
                    sem = gr_r + slot * (4 * SPLIT) + q * (2 * SPLIT) + j
                    send(gs.at[m, r], gr.at[slot, r], gr_si[q][m], sem, dev(dz=e["back"]))

    def finish(q):
        for j in range(2 * SPLIT):
            i = q * 2 * SPLIT + j
            r = slice(i * SUB, i * SUB + SUB)

            @pl.when(home)
            def _():
                lg[...] = term[q, mine, j * SUB : j * SUB + SUB, :]

            @pl.when(home_up)
            def _():
                arrived(gr.at[mine, r], gr_r + mine * (4 * SPLIT) + i)
                lg[...] += gr[mine, r, :].astype(F32)

            @pl.when(home_dn)
            def _():
                arrived(gr.at[4, r], gr_r + 16 * SPLIT + i)
                lg[...] += gr[4, r, :].astype(F32)

            @pl.when(home)
            def _():
                grad = lg[...] * gp[r, :]
                pg[r, :] = grad.astype(BF)
                total = jnp.sum(grad, axis=0, keepdims=True)
                if i == 0:
                    bs[...] = jnp.broadcast_to(total, (8, 256))
                else:
                    bs[...] += jnp.broadcast_to(total, (8, 256))
                send(pg.at[r], pg.at[r], pg_si, pg_r + i, mate)

    def flip_inputs(q, j):
        kk = k if j == 0 else 1 - k
        for i in range(2):
            block = xp[q, kk, :, :, :, :, i * 1024 : i * 1024 + 1024].reshape(128, 1024)
            xt[i * 1024 : i * 1024 + 1024, rows(q, j)] = block.T

    def flip_latents(q):
        for m in range(4):
            lt[m * 256 : m * 256 + 256, q * 256 : q * 256 + 256] = latb[m, q * 256 : q * 256 + 256, :].T

    dec_copies, dec_sem = {}, [lnum.take(), lnum.take()]

    def dec_part(i):
        ab, hh = i // 2, i % 2
        if i >= 2:
            dec_copies[i - 2].wait()

        right = err[:, :, :, :, :, :, i * 512 : i * 512 + 512].reshape(512, 512)
        dg[i % 2] = jnp.dot(lt[...], right, preferred_element_type=F32).astype(BF)
        start = hh * 1024 + ab * 512
        dec_copies[i] = local(dg.at[i % 2], dec_hbm.at[:, start : start + 512], dec_sem[i % 2])

    load_we.wait()
    load_b.wait()
    encode(0)
    pl.semaphore_wait(barrier, len(peers))
    first_send(0)
    encode(1)
    load_w = lnum.take()
    for ab in range(2):
        for hh in range(2):
            local(
                w_hbm.at[:, hh * 1024 + ab * 512 : hh * 1024 + ab * 512 + 512],
                wp.at[:, ab * 1024 + hh * 512 : ab * 1024 + hh * 512 + 512],
                load_w,
            )
    clear()
    lat_hop(0, 0)
    lat_hop(0, 1)
    first_send(1)
    send_inputs()
    flip_inputs(0, 0)
    lat_hop(0, 2)
    lat_hop(1, 0)
    lat_hop(1, 1)
    lat_hop(0, 3)
    flip_inputs(1, 0)
    lat_hop(1, 2)
    lat_last(0)
    landed(wp, load_w)
    decode(0, 0)
    lat_hop(1, 3)
    decode(0, 1)
    stage_a(0)
    flip_latents(0)
    lat_last(1)
    decode(1, 0)
    decode(1, 1)
    stage_b(0)
    flip_latents(1)
    stage_a(1)
    arrived(tg.at[1 - k], mate_t)
    stage_c(0)
    stage_b(1)
    arrived(xp.at[c, 1 - k], mate_x)
    send(xp.at[c, 1 - k], xp.at[c, 1 - k], group(xp.at[c, 1 - k]), core_x, dev(flip=1))
    stage_d(0)
    stage_c(1)
    stage_e(0)
    arrived(xp.at[o, 1 - k], core_x)
    for q in range(2):
        gp[rows(q, 1), :] = preact(q, 1 - k)[1]
    flip_inputs(0, 1)
    stage_d(1)
    stage_f(0)
    grad_step(0, 0)
    flip_inputs(1, 1)
    xt_copy = local(xt, xt_hbm)
    recs[:, pl.ds(mul(k, 1024), 1024)] = rc[k]
    send(rc.at[1 - k], recs.at[:, pl.ds(mul(k, 1024), 1024)], group(rc.at[1 - k]), mate_rec, mate)
    grad_step(0, 1)
    stage_e(1)
    grad_step(0, 2)
    stage_f(1)
    grad_step(1, 0)
    grad_step(0, 3)
    dec_part(0)
    grad_step(1, 1)
    finish(0)
    dec_part(1)
    grad_step(1, 2)
    dec_part(2)
    grad_step(1, 3)
    dec_part(3)
    finish(1)
    send(bs, bs, group(bs, home), mate_bias, mate, home)
    for i in range(4 * SPLIT):
        arrived(pg.at[i * SUB : i * SUB + SUB], pg_r + i, away)

    pg_copy = local(pg, pg_hbm)
    arrived(bs, mate_bias, away)
    bias_copy = local(bs.at[0:1], bias_hbm)
    arrived(recs.at[:, pl.ds(mul(1 - k, 1024), 1024)], mate_rec)
    rec_copy = local(recs, rec_hbm)
    for si, like, cond in sent:
        copy = rc_(like, like, si, 0, mate)
        if cond is None:
            copy.wait_send()
        else:
            pl.when(cond)(copy.wait_send)
    dec_copies[2].wait()
    dec_copies[3].wait()
    for copy in (xt_copy, pg_copy, bias_copy, rec_copy):
        copy.wait()
    assert (snum.count, rnum.count, lnum.count) == COUNTS, (snum.count, rnum.count, lnum.count)


def outputs(rec_in, bias_in, pg_hbm, xt_hbm, dec_in, rec, enc, bias, dec, recv, biasv, pg, xt, encv, decv, sem):
    def part(i):
        return pl.ds(i * 256, 256)

    loads = [pltpu.make_async_copy(pg_hbm, pg, sem.at[0]), pltpu.make_async_copy(xt_hbm, xt, sem.at[1])]
    dec_loads = [pltpu.make_async_copy(dec_in.at[part(i)], decv.at[part(i)], sem.at[2 + i]) for i in range(4)]
    dec_stores = [pltpu.make_async_copy(decv.at[part(i)], dec.at[part(i)], sem.at[6 + i]) for i in range(4)]
    enc_store = pltpu.make_async_copy(encv, enc, sem.at[10])
    small_loads = [pltpu.make_async_copy(rec_in, recv, sem.at[11]), pltpu.make_async_copy(bias_in, biasv, sem.at[12])]
    small_stores = [pltpu.make_async_copy(recv, rec, sem.at[13]), pltpu.make_async_copy(biasv, bias, sem.at[14])]
    for copy in loads + dec_loads + small_loads:
        copy.start()
    for copy in loads:
        copy.wait()
    for i in range(2):
        dec_loads[i].wait()
        dec_stores[i].start()
    encv[...] = jnp.dot(xt[...], pg[...], preferred_element_type=F32).astype(BF)
    enc_store.start()
    for i in range(2, 4):
        dec_loads[i].wait()
        dec_stores[i].start()
    for load, store in zip(small_loads, small_stores):
        load.wait()
        store.start()
    for copy in dec_stores + small_stores + [enc_store]:
        copy.wait()


def kernel1(layer_inputs, layer_targets, encoder_weight, encoder_bias, decoder_weight):
    vm, hbm = pl.BlockSpec(memory_space=pltpu.VMEM), pl.BlockSpec(memory_space=pl.ANY)
    scratch = [
        pltpu.VMEM((16, 2048), BF),
        pltpu.VMEM((1, 256), F32),
        pltpu.VMEM((2, 2, 2, 2, 2, 16, 2048), BF),
        pltpu.VMEM((2048, 512), BF),
        pltpu.VMEM((2048, 256), BF),
        pltpu.VMEM((1024, 2048), BF),
        pltpu.VMEM((2, 128, 256), BF),
        pltpu.VMEM((5, 512, 256), BF),
        pltpu.VMEM((1024, 512), BF),
        pltpu.VMEM((512, 256), F32),
        pltpu.VMEM((2, 16, 1024), BF),
        pltpu.VMEM((2, 2, 2, 64, 1024), F32),
        pltpu.VMEM((2, 2, 2, 64, 1024), BF),
        pltpu.VMEM((2, 2, 2, 64, 1024), BF),
        pltpu.VMEM((2, 4, 2, 16, 1024), F32),
        pltpu.VMEM((2, 2, 4, 2, 16, 1024), BF),
        pltpu.VMEM((2, 3, 4, 16, 512), BF),
        pltpu.VMEM((2, 3, 2, 16, 1024), BF),
        pltpu.VMEM((2, 4, 16, 512), F32),
        pltpu.VMEM((2, 2, 4, 16, 512), BF),
        pltpu.VMEM((2, 2, 3, 16, 512), BF),
        pltpu.VMEM((2, 16, 1024), BF),
        pltpu.VMEM((2, 2, 2, 2, 2, 16, 2048), BF),
        pltpu.VMEM((2, 4, 256, 256), F32),
        pltpu.VMEM((5, 512, 256), BF),
        pltpu.VMEM((4, 512, 256), BF),
        pltpu.VMEM((SUB, 256), F32),
        pltpu.VMEM((512, 256), BF),
        pltpu.VMEM((8, 256), F32),
        pltpu.VMEM((16, 2048), BF),
        pltpu.VMEM((2, 1024, 512), BF),
        *[pltpu.SemaphoreType.DMA((n,)) for n in COUNTS],
    ]
    rec, bias, pg, xt, dec = pl.pallas_call(
        kernel,
        out_shape=(
            jax.ShapeDtypeStruct((16, 2048), BF),
            jax.ShapeDtypeStruct((1, 256), F32),
            jax.ShapeDtypeStruct((512, 256), BF),
            jax.ShapeDtypeStruct((2048, 512), BF),
            jax.ShapeDtypeStruct((1024, 2048), BF),
        ),
        in_specs=[hbm] * 5,
        out_specs=[hbm] * 5,
        scratch_shapes=scratch,
        compiler_params=pltpu.CompilerParams(
            collective_id=0, has_side_effects=True, vmem_limit_bytes=56 * 1024 * 1024
        ),
        name="transcoder_step",
    )(
        layer_inputs.reshape(2, 2, 2, 2, 16, 2048),
        layer_targets[0],
        encoder_weight[0],
        encoder_bias,
        decoder_weight.reshape(1024, 2048),
    )
    return rec, bias, pg, xt, dec


def shards(*args):
    vm, hbm = pl.BlockSpec(memory_space=pltpu.VMEM), pl.BlockSpec(memory_space=pl.ANY)
    rec, bias, pg, xt, dec = kernel1(*args)
    rec, enc, bias, dec = pl.pallas_call(
        outputs,
        out_shape=(
            jax.ShapeDtypeStruct((16, 2048), BF),
            jax.ShapeDtypeStruct((2048, 256), BF),
            jax.ShapeDtypeStruct((1, 256), F32),
            jax.ShapeDtypeStruct((1024, 2048), BF),
        ),
        in_specs=[hbm] * 5,
        out_specs=[hbm] * 4,
        scratch_shapes=[
            pltpu.VMEM((16, 2048), BF),
            pltpu.VMEM((1, 256), F32),
            pltpu.VMEM((512, 256), BF),
            pltpu.VMEM((2048, 512), BF),
            pltpu.VMEM((2048, 256), BF),
            pltpu.VMEM((1024, 2048), BF),
            pltpu.SemaphoreType.DMA((15,)),
        ],
        compiler_params=pltpu.CompilerParams(vmem_limit_bytes=56 * 1024 * 1024),
        name="write_outputs",
    )(rec, bias, pg, xt, dec)
    return rec[None], enc[None], bias, dec.reshape(1, 4, 1, 256, 2048)


def solution(mesh):
    placed = (
        P("layer", "tok", None),
        P("layer", ("latent", "tok"), None),
        P("layer", None, "latent"),
        P("layer", "latent"),
        P("layer", None, "tok", "latent", None),
    )
    return jax.shard_map(
        shards,
        mesh=mesh,
        in_specs=placed,
        out_specs=(
            P("layer", ("latent", "tok"), None),
            P("layer", None, "latent"),
            P("layer", "latent"),
            P("layer", None, "tok", "latent", None),
        ),
        check_vma=False,
    )
```

time: 99.7 us -> 85.2 us (0.85)
  local copies, waits for them, and re-layouts: 9.74 us -> 0 us
  Pallas kernels: 89.1 us -> 84.4 us
    unnamed x4 -> x0, local copies, waits for them, and re-layouts: 9.74 us -> none
    pallas_call x1 -> x2, Pallas kernels: 89.1 us -> 84.4 us  [the longest x1 79.7 us: kernel1(): pl.pallas_call(kernel, out_shape=(jax.ShapeDtypeStruct((16, 2048), BF), j...]
where the time goes in v2:
time: 85.2 us; the launch traced here: 85.1 us
  Pallas kernels  84.4 us (99%)
    pallas_call x1, Pallas kernels, kernel1(): pl.pallas_call(kernel, out_shape=(jax.ShapeDtypeStruct((16, 2048), BF), j...  79.7 us
    pallas_call x1, Pallas kernels, shards(): pl.pallas_call(outputs, out_shape=(jax.ShapeDtypeStruct((16, 2048), BF),...  4.77 us

profile of v2, /device:TPU:8, one launch (start us, length us, event | category | flops | bytes accessed | tf_op | source)
XLA Modules:
  0.0 85.1 jit_solution(1008562218983902833)
XLA Ops:
  0.6 79.7 %transcoder_step.1 = (bf16[16,2048]{1,0:T(8,128)(2,1)}, f32[1,256]{1,0:T(1,128)}, bf16[512,256]{1,0:T(8,128)(2,1)}, bf16[2048,512]{1,0:T(8,128)(2,1)}, bf16[1024,2048]{1,0:T(8,128)(2,1)}) custom-call(bf16[2,2,2,2,16,2048]{5,4,3,2,1,0:T(8,128)(2,1)} %bitcast.10, bf16[16,2048]{1,0:T(8,128)(2,1)} %bitcast.12, bf16[2048,256]{1,0:T(8,128)(2,1)} %bitcast.11, ...), custom_call_target="tpu_custom_call" | custom-call | tf_op jit(solution)/shard_map/transcoder_step/pallas_call | solution.py:569
  80.3 4.8 %write_outputs.1 = (bf16[16,2048]{1,0:T(8,128)(2,1)}, bf16[2048,256]{1,0:T(8,128)(2,1)}, f32[1,256]{1,0:T(1,128)}, bf16[1024,2048]{1,0:T(8,128)(2,1)}) custom-call(bf16[16,2048]{1,0:T(8,128)(2,1)} %get-tuple-element.13.rec_in, f32[1,256]{1,0:T(1,128)} %get-tuple-element.14.bias_in, bf16[512,256]{1,0:T(8,128)(2,1)} %get-tuple-element.15.pg_hbm, ...), custom_call_target="tpu_custom_call" | custom-call | tf_op jit(solution)/shard_map/write_outputs/pallas_call | solution.py:598

commit v3 on v2

--- a/solution.py
+++ b/solution.py
@@ -8,7 +8,7 @@
 MESH = pl.DeviceIdType.MESH
 SPLIT = 2
 SUB = 128 // SPLIT
-COUNTS = (47, 109, 12)
+COUNTS = (45, 113, 12)
 BF = jnp.bfloat16
 F32 = jnp.float32
 
@@ -94,6 +94,9 @@
     barrier = pltpu.get_barrier_semaphore()
     peers = [dev(dz=1), dev(dz=-1), dev(flip=1)]
     peers += [dev(dy=d) for d in (1, 2, 3)] + [dev(dx=d) for d in (1, 2, 3)]
+    across = [((z + 1) % 8, lat, 1 - k), ((z + 7) % 8, lat, 1 - k)]
+    across_x = [(z, (x + d) % 4 * 4 + yh * 2 + c, 1 - k) for d in (1, 2, 3)]
+    peers += across + across_x
     for to in peers:
         pl.semaphore_signal(barrier, inc=1, device_id=to, device_id_type=MESH)
 
@@ -116,11 +119,13 @@
                           onward=jnp.where(on_up, 1, 7), back=jnp.where(on_up, 7, 1)))
     mine = z // 2
     home = k == h
-    ku_own = jnp.where(mine == 0, 4, jnp.where(mine == 1, 4, jnp.where(mine == 2, 3 - k, 1 - k)))
-    kd_own = jnp.where(mine == 0, 3, jnp.where(mine == 1, 3 * (1 - k), 0))
+    ku_own = jnp.where(mine == 0, 4, jnp.where(mine == 1, 4, jnp.where(mine == 2, 3 - h, 1 - h)))
+    kd_own = jnp.where(mine == 0, 3, jnp.where(mine == 1, 3 * (1 - h), 0))
     home_up = jnp.logical_and(home, ku_own > 0)
     home_dn = jnp.logical_and(home, kd_own > 0)
     away = jnp.logical_not(home)
+    away_up = jnp.logical_and(away, ku_own > 0)
+    away_dn = jnp.logical_and(away, kd_own > 0)
 
     def clear():
         for m in range(4):
@@ -144,8 +149,9 @@
         kk = k if j < SPLIT else 1 - k
         return pl.ds(pl.multiple_of(q * 256 + kk * 128 + (j % SPLIT) * SUB, SUB), SUB)
 
-    up_si, dn_si = group(latb.at[0], home_up), group(latb.at[0], home_dn)
+    up_si, dn_si = group(own, home_up), group(own, home_dn)
     away_si, pg_si = group(own, away), group(pg, home)
+    away_up_si, away_dn_si = group(own, away_up), group(own, away_dn)
     lat_si = [[snum.take() for m in range(3)] for q in range(2)]
     gr_si = [[snum.take() for m in range(4)] for q in range(2)]
 
@@ -181,21 +187,32 @@
     def first_send(q):
         for j in range(SPLIT):
             src = own.at[q, j * SUB : j * SUB + SUB]
-            send(src, latb.at[mine, some(q, j)], away_si, lat_sem(mine, q, SPLIT + j), mate, away)
+            dst, sem = latb.at[mine, some(q, j)], lat_sem(mine, q, SPLIT + j)
+            dn_dst = latb.at[jnp.where(z >= 1, 4, mine), some(q, j)]
+            send(src, dst, away_up_si, sem, across[0], away_up)
+            send(src, dn_dst, away_dn_si, sem, across[1], away_dn)
+            send(src, dst, away_si, sem, mate, away)
             origin_send(q, j)
 
     def send_inputs():
         load_t.wait()
-        tg[k] = t_ref[:, pl.ds(mul(k, 1024), 1024)]
-        send(t_ref.at[:, pl.ds(mul(1 - k, 1024), 1024)], tg.at[k], group(tg.at[k]), mate_t, mate)
+        tg[pl.ds(k * 4 + x, 1)] = t_ref[:, pl.ds(mul(k, 1024), 512)][None]
+        for hh in range(2):
+            at = 8 + (k * 2 + yh) * 2 + hh
+            tg[pl.ds(at, 1)] = t_ref[:, hh * 1024 + 512 : hh * 1024 + 1024][None]
+        si = group(tg.at[0:13])
+        slot = tg.at[k * 4 + x]
+        here, there = pl.ds(mul(k, 1024), 512), pl.ds(mul(1 - k, 1024), 512)
+        for d in (1, 2, 3):
+            send(t_ref.at[:, here], slot, si, mate_t, dev(dx=d))
+            send(t_ref.at[:, there], slot, si, mate_t, across_x[d - 1])
+            for hh in range(2):
+                at = 8 + (k * 2 + yh) * 2 + hh
+                send(t_ref.at[:, hh * 1024 + 512 : hh * 1024 + 1024], tg.at[at], si, mate_t, dev(dy=d))
+        send(t_ref.at[:, there], slot, si, mate_t, mate)
         send(xp.at[c, k], xp.at[c, k], group(xp.at[c, k]), mate_x, mate)
 
     def lat_hop(q, far):
-        if far == 0:
-            for j in range(SPLIT, 2 * SPLIT):
-                arrived(latb.at[mine, some(q, j)], lat_sem(mine, q, j), home)
-                origin_send(q, j)
-            return
         conds = []
         for m in range(3):
             e = route[m]
@@ -226,23 +243,28 @@
                 for j in range(2 * SPLIT):
                     arrived(latb.at[m, some(q, j)], lat_sem(m, q, j))
 
+        @pl.when(home)
+        def _():
+            for j in range(SPLIT, 2 * SPLIT):
+                arrived(latb.at[mine, some(q, j)], lat_sem(mine, q, j))
+
     piece = {}
     for q in range(2):
         for ab in range(2):
-            piece[q, ab] = {name: rnum.take() for name in ("core", "a", "b", "g1", "g2", "g3")}
+            piece[q, ab] = {"core": rnum.take(), "a": rnum.take(), "b": rnum.take(), "g2": rnum.take(3), "g3": rnum.take()}
 
     def decode(q, ab):
         left = jnp.concatenate([latb[m, q * 256 : q * 256 + 256, :] for m in range(4)], axis=1)
         part = jnp.dot(left, wp[:, ab * 1024 : ab * 1024 + 1024], preferred_element_type=F32)
-        p32[ab] = part.reshape(2, 2, 64, 1024)
-        cs[q, ab] = p32[ab, :, o].astype(BF)
+        p32[q, ab] = part.reshape(2, 2, 64, 1024)
+        cs[q, ab] = p32[q, ab, :, o].astype(BF)
         send(cs.at[q, ab], cr.at[q, ab], group(cs.at[q, ab]), piece[q, ab]["core"], dev(flip=1))
 
     def stage_a(q):
         for ab in range(2):
             arrived(cr.at[q, ab], piece[q, ab]["core"])
-            total = (p32[ab, :, c] + cr[q, ab].astype(F32)).reshape(4, 2, 16, 1024)
-            s32[ab] = total
+            total = (p32[q, ab, :, c] + cr[q, ab].astype(F32)).reshape(4, 2, 16, 1024)
+            s32[q, ab] = total
             ys[q, ab] = total.astype(BF)
             wide = ra.at[q] if ab == 0 else rb.at[q]
             si, sem = group(wide), piece[q, ab]["a"]
@@ -259,29 +281,23 @@
             buf = ra if ab == 0 else rb
             arrived(buf.at[q], piece[q, ab]["a"])
             if ab == 0:
-                total = s32[0, :, yh, :, pl.ds(mul(k, 512), 512)]
+                total = s32[q, 0, :, yh, :, pl.ds(mul(k, 512), 512)]
             else:
-                total = s32[1, x]
+                total = s32[q, 1, x]
             for d in range(3):
                 total = total + buf[q, d].astype(F32)
             if ab == 0:
-                u32[0] = total
+                u32[q, 0] = total
                 xs[q, 0] = total.astype(BF)
             else:
                 for yy in range(4):
                     block = total[yy // 2, :, (yy % 2) * 512 : (yy % 2) * 512 + 512]
-                    u32[1, yy] = block
+                    u32[q, 1, yy] = block
                     xs[q, 1, yy] = block.astype(BF)
             si, sem = group(rx.at[q, ab]), piece[q, ab]["b"]
             for d in (1, 2, 3):
-                if ab == 0:
-                    send(xs.at[q, 0, (x + d) % 4], rx.at[q, 0, d - 1], si, sem, dev(dx=d))
-                else:
-                    send(xs.at[q, 1, (y + d) % 4], rx.at[q, 1, d - 1], si, sem, dev(dy=d))
-
-    def block_of(q, ab, xx, yy):
-        cols = pl.ds(pl.multiple_of(ab * 1024 + (yy % 2) * 512, 512), 512)
-        return err.at[q, xx // 2, c, xx % 2, yy // 2, :, cols]
+                to = dev(dx=d) if ab == 0 else dev(dy=d)
+                send(xs.at[q, ab], rx.at[q, ab, d - 1], si, sem, to)
 
     def line_of(q, ab, xx, yy):
         if ab == 0:
@@ -292,33 +308,38 @@
     def stage_c(q):
         for ab in range(2):
             arrived(rx.at[q, ab], piece[q, ab]["b"])
-            total = u32[ab, x if ab == 0 else y]
+            total = u32[q, ab]
             for d in range(3):
                 total = total + rx[q, ab, d].astype(F32)
-            rc[q, :, ab * 512 : ab * 512 + 512] = total.astype(BF)
-            diff = total - tg[q, :, ab * 512 : ab * 512 + 512].astype(F32)
-            cols = pl.ds(pl.multiple_of(ab * 1024 + k * 512, 512), 512)
-            err[q, x // 2, c, x % 2, yh, :, cols] = diff.astype(BF)
-            mine_ = block_of(q, ab, x, y)
-            si = group(rx.at[q, ab])
-            for d in (1, 2, 3):
-                to = dev(dx=d) if ab == 0 else dev(dy=d)
-                send(mine_, mine_, si, piece[q, ab]["g1"], to)
-
-    def stage_d(q):
-        for ab in range(2):
-            arrived(rx.at[q, ab], piece[q, ab]["g1"])
+            u32[q, ab] = total
+            if ab == 0:
+                diff = (total - tg[q * 4 : q * 4 + 4].astype(F32)).astype(BF)
+                cols = pl.ds(mul(k, 512), 512)
+                for xx in range(4):
+                    err[q, xx // 2, c, xx % 2, yh, :, cols] = diff[xx]
+            else:
+                diff = (total - tg[8 + q * 4 : 12 + q * 4].astype(F32)).astype(BF)
+                for yy in range(4):
+                    start = 1024 + (yy % 2) * 512
+                    err[q, x // 2, c, x % 2, yy // 2, :, start : start + 512] = diff[yy]
             line = line_of(q, ab, x, y)
             si = group(ra.at[q])
             for d in (1, 2, 3):
                 to = dev(dy=d) if ab == 0 else dev(dx=d)
-                send(line, line, si, piece[q, ab]["g2"], to)
+                send(line, line, si, piece[q, ab]["g2"] + d - 1, to)
+            half = err.at[q, :, c, :, :, :, ab * 1024 : ab * 1024 + 1024]
+            core_si[q, ab] = group(half)
+            send(line, line, core_si[q, ab], piece[q, ab]["g3"], dev(flip=1))
+            rc[q, :, ab * 512 : ab * 512 + 512] = u32[q, ab, x if ab == 0 else y].astype(BF)
+
+    core_si = {}
 
     def stage_e(q):
-        for ab in range(2):
-            arrived(ra.at[q], piece[q, ab]["g2"])
-            half = err.at[q, :, c, :, :, :, ab * 1024 : ab * 1024 + 1024]
-            send(half, half, group(half), piece[q, ab]["g3"], dev(flip=1))
+        for d in (1, 3, 2):
+            for ab in range(2):
+                line = line_of(q, ab, (x - d + 4) % 4, (y - d + 4) % 4)
+                arrived(line, piece[q, ab]["g2"] + d - 1)
+                send(line, line, core_si[q, ab], piece[q, ab]["g3"], dev(flip=1))
 
     def stage_f(q):
         for ab in range(2):
@@ -331,9 +352,10 @@
             )
             term[q, 2 * half] = out[:, :256]
             term[q, 2 * half + 1] = out[:, 256:]
-
-    def grad_step(q, depth):
-        for m in range(4):
+            grad_step(q, 0, (2 * half, 2 * half + 1))
+
+    def grad_step(q, depth, members=range(4)):
+        for m in members:
             if depth > (3, 3, 2, 0)[m]:
                 continue
             e = route[m]
@@ -394,17 +416,22 @@
         for m in range(4):
             lt[m * 256 : m * 256 + 256, q * 256 : q * 256 + 256] = latb[m, q * 256 : q * 256 + 256, :].T
 
-    dec_copies, dec_sem = {}, [lnum.take(), lnum.take()]
-
-    def dec_part(i):
-        ab, hh = i // 2, i % 2
-        if i >= 2:
-            dec_copies[i - 2].wait()
-
-        right = err[:, :, :, :, :, :, i * 512 : i * 512 + 512].reshape(512, 512)
-        dg[i % 2] = jnp.dot(lt[...], right, preferred_element_type=F32).astype(BF)
-        start = hh * 1024 + ab * 512
-        dec_copies[i] = local(dg.at[i % 2], dec_hbm.at[:, start : start + 512], dec_sem[i % 2])
+    dec_sem = lnum.take()
+    lnum.take()
+
+    def dec_store(i):
+        start = pl.multiple_of((i % 2) * 1024 + (i // 2) * 512, 512)
+        return pltpu.make_async_copy(dg.at[i % 2], dec_hbm.at[:, pl.ds(start, 512)], ls.at[dec_sem + i % 2])
+
+    def decoder_grads():
+        def part(i, _):
+            pl.when(i >= 2)(lambda: dec_store(i - 2).wait())
+            right = err[:, :, :, :, :, :, pl.ds(mul(i, 512), 512)].reshape(512, 512)
+            dg[i % 2] = jnp.dot(lt[...], right, preferred_element_type=F32).astype(BF)
+            dec_store(i).start()
+            return 0
+
+        lax.fori_loop(0, 4, part, 0)
 
     load_we.wait()
     load_b.wait()
@@ -412,6 +439,7 @@
     pl.semaphore_wait(barrier, len(peers))
     first_send(0)
     encode(1)
+    first_send(1)
     load_w = lnum.take()
     for ab in range(2):
         for hh in range(2):
@@ -420,64 +448,55 @@
                 wp.at[:, ab * 1024 + hh * 512 : ab * 1024 + hh * 512 + 512],
                 load_w,
             )
+    send_inputs()
     clear()
-    lat_hop(0, 0)
     lat_hop(0, 1)
-    first_send(1)
-    send_inputs()
+    lat_hop(1, 1)
     flip_inputs(0, 0)
     lat_hop(0, 2)
-    lat_hop(1, 0)
-    lat_hop(1, 1)
+    lat_hop(1, 2)
+    flip_inputs(1, 0)
     lat_hop(0, 3)
-    flip_inputs(1, 0)
-    lat_hop(1, 2)
+    lat_hop(1, 3)
     lat_last(0)
     landed(wp, load_w)
     decode(0, 0)
-    lat_hop(1, 3)
     decode(0, 1)
-    stage_a(0)
-    flip_latents(0)
     lat_last(1)
     decode(1, 0)
+    stage_a(0)
     decode(1, 1)
-    stage_b(0)
+    flip_latents(0)
+    stage_a(1)
     flip_latents(1)
-    stage_a(1)
-    arrived(tg.at[1 - k], mate_t)
-    stage_c(0)
-    stage_b(1)
     arrived(xp.at[c, 1 - k], mate_x)
     send(xp.at[c, 1 - k], xp.at[c, 1 - k], group(xp.at[c, 1 - k]), core_x, dev(flip=1))
-    stage_d(0)
-    stage_c(1)
-    stage_e(0)
+    stage_b(0)
+    stage_b(1)
+    arrived(tg.at[0:13], mate_t)
     arrived(xp.at[o, 1 - k], core_x)
     for q in range(2):
         gp[rows(q, 1), :] = preact(q, 1 - k)[1]
+    stage_c(0)
+    stage_c(1)
     flip_inputs(0, 1)
-    stage_d(1)
-    stage_f(0)
-    grad_step(0, 0)
     flip_inputs(1, 1)
     xt_copy = local(xt, xt_hbm)
+    stage_e(0)
+    stage_e(1)
+    stage_f(0)
+    stage_f(1)
     recs[:, pl.ds(mul(k, 1024), 1024)] = rc[k]
     send(rc.at[1 - k], recs.at[:, pl.ds(mul(k, 1024), 1024)], group(rc.at[1 - k]), mate_rec, mate)
+    pl.when(z < 4)(decoder_grads)
     grad_step(0, 1)
-    stage_e(1)
+    grad_step(1, 1)
     grad_step(0, 2)
-    stage_f(1)
-    grad_step(1, 0)
+    grad_step(1, 2)
     grad_step(0, 3)
-    dec_part(0)
-    grad_step(1, 1)
+    grad_step(1, 3)
+    pl.when(z >= 4)(decoder_grads)
     finish(0)
-    dec_part(1)
-    grad_step(1, 2)
-    dec_part(2)
-    grad_step(1, 3)
-    dec_part(3)
     finish(1)
     send(bs, bs, group(bs, home), mate_bias, mate, home)
     for i in range(4 * SPLIT):
@@ -494,8 +513,8 @@
             copy.wait_send()
         else:
             pl.when(cond)(copy.wait_send)
-    dec_copies[2].wait()
-    dec_copies[3].wait()
+    dec_store(2).wait()
+    dec_store(3).wait()
     for copy in (xt_copy, pg_copy, bias_copy, rec_copy):
         copy.wait()
     assert (snum.count, rnum.count, lnum.count) == COUNTS, (snum.count, rnum.count, lnum.count)
@@ -543,17 +562,17 @@
         pltpu.VMEM((5, 512, 256), BF),
         pltpu.VMEM((1024, 512), BF),
         pltpu.VMEM((512, 256), F32),
-        pltpu.VMEM((2, 16, 1024), BF),
-        pltpu.VMEM((2, 2, 2, 64, 1024), F32),
+        pltpu.VMEM((16, 16, 512), BF),
+        pltpu.VMEM((2, 2, 2, 2, 64, 1024), F32),
         pltpu.VMEM((2, 2, 2, 64, 1024), BF),
         pltpu.VMEM((2, 2, 2, 64, 1024), BF),
-        pltpu.VMEM((2, 4, 2, 16, 1024), F32),
+        pltpu.VMEM((2, 2, 4, 2, 16, 1024), F32),
         pltpu.VMEM((2, 2, 4, 2, 16, 1024), BF),
         pltpu.VMEM((2, 3, 4, 16, 512), BF),
         pltpu.VMEM((2, 3, 2, 16, 1024), BF),
-        pltpu.VMEM((2, 4, 16, 512), F32),
+        pltpu.VMEM((2, 2, 4, 16, 512), F32),
         pltpu.VMEM((2, 2, 4, 16, 512), BF),
-        pltpu.VMEM((2, 2, 3, 16, 512), BF),
+        pltpu.VMEM((2, 2, 3, 4, 16, 512), BF),
         pltpu.VMEM((2, 16, 1024), BF),
         pltpu.VMEM((2, 2, 2, 2, 2, 16, 2048), BF),
         pltpu.VMEM((2, 4, 256, 256), F32),

time: 85.2 us -> 76.5 us (0.90)
  Pallas kernels: 84.4 us -> 75.2 us
    pallas_call x1, Pallas kernels: 79.7 us -> 70.4 us  [kernel1(): pl.pallas_call(kernel, out_shape=(jax.ShapeDtypeStruct((16, 2048), BF), j...]
where the time goes in v3:
time: 76.5 us; the launch traced here: 75.8 us
  Pallas kernels  75.2 us (98%)
    pallas_call x1, Pallas kernels, kernel1(): pl.pallas_call(kernel, out_shape=(jax.ShapeDtypeStruct((16, 2048), BF), j...  70.4 us
    pallas_call x1, Pallas kernels, shards(): pl.pallas_call(outputs, out_shape=(jax.ShapeDtypeStruct((16, 2048), BF),...  4.77 us

profile of v3, /device:TPU:8, one launch (start us, length us, event | category | flops | bytes accessed | tf_op | source)
XLA Modules:
  0.0 75.8 jit_solution(924073169028445273)
XLA Ops:
  0.6 70.4 %transcoder_step.1 = (bf16[16,2048]{1,0:T(8,128)(2,1)}, f32[1,256]{1,0:T(1,128)}, bf16[512,256]{1,0:T(8,128)(2,1)}, bf16[2048,512]{1,0:T(8,128)(2,1)}, bf16[1024,2048]{1,0:T(8,128)(2,1)}) custom-call(bf16[2,2,2,2,16,2048]{5,4,3,2,1,0:T(8,128)(2,1)} %bitcast.10, bf16[16,2048]{1,0:T(8,128)(2,1)} %bitcast.12, bf16[2048,256]{1,0:T(8,128)(2,1)} %bitcast.11, ...), custom_call_target="tpu_custom_call" | custom-call | tf_op jit(solution)/shard_map/transcoder_step/pallas_call | solution.py:588
  71.1 4.8 %write_outputs.1 = (bf16[16,2048]{1,0:T(8,128)(2,1)}, bf16[2048,256]{1,0:T(8,128)(2,1)}, f32[1,256]{1,0:T(1,128)}, bf16[1024,2048]{1,0:T(8,128)(2,1)}) custom-call(bf16[16,2048]{1,0:T(8,128)(2,1)} %get-tuple-element.13.rec_in, f32[1,256]{1,0:T(1,128)} %get-tuple-element.14.bias_in, bf16[512,256]{1,0:T(8,128)(2,1)} %get-tuple-element.15.pg_hbm, ...), custom_call_target="tpu_custom_call" | custom-call | tf_op jit(solution)/shard_map/write_outputs/pallas_call | solution.py:617

commit v4 on v3

--- a/solution.py
+++ b/solution.py
@@ -8,7 +8,7 @@
 MESH = pl.DeviceIdType.MESH
 SPLIT = 2
 SUB = 128 // SPLIT
-COUNTS = (45, 113, 12)
+COUNTS = (45, 113, 6)
 BF = jnp.bfloat16
 F32 = jnp.float32
 
@@ -29,9 +29,9 @@
 
 def kernel(
     x_hbm, t_hbm, we_hbm, b_hbm, w_hbm,
-    rec_hbm, bias_hbm, pg_hbm, xt_hbm, dec_hbm,
-    t_ref, b_ref,    xp, xt, we, wp, own, latb, lt, gp, tg, p32, cs, cr, s32, ys, ra, rb, u32, xs, rx, rc, err,
-    term, gr, gs, lg, pg, bs, recs, dg, ss, rs, ls,
+    rec_out, bias_out, pg_out, xt, dec_out,
+    t_ref, b_ref, xp, we, wp, own, latb, lt, gp, tg, p32, cs, cr, s32, ys, ra, rb, u32, xs, rx, rc, err,
+    term, gr, gs, lg, pg, bs, recs, ss, rs, ls,
 ):
     z, lat, k = lax.axis_index("layer"), lax.axis_index("latent"), lax.axis_index("tok")
     x, yh, c = lat // 4, (lat // 2) % 2, lat % 2
@@ -416,19 +416,11 @@
         for m in range(4):
             lt[m * 256 : m * 256 + 256, q * 256 : q * 256 + 256] = latb[m, q * 256 : q * 256 + 256, :].T
 
-    dec_sem = lnum.take()
-    lnum.take()
-
-    def dec_store(i):
-        start = pl.multiple_of((i % 2) * 1024 + (i // 2) * 512, 512)
-        return pltpu.make_async_copy(dg.at[i % 2], dec_hbm.at[:, pl.ds(start, 512)], ls.at[dec_sem + i % 2])
-
     def decoder_grads():
         def part(i, _):
-            pl.when(i >= 2)(lambda: dec_store(i - 2).wait())
             right = err[:, :, :, :, :, :, pl.ds(mul(i, 512), 512)].reshape(512, 512)
-            dg[i % 2] = jnp.dot(lt[...], right, preferred_element_type=F32).astype(BF)
-            dec_store(i).start()
+            start = pl.multiple_of((i % 2) * 1024 + (i // 2) * 512, 512)
+            dec_out[:, pl.ds(start, 512)] = jnp.dot(lt[...], right, preferred_element_type=F32).astype(BF)
             return 0
 
         lax.fori_loop(0, 4, part, 0)
@@ -481,7 +473,6 @@
     stage_c(1)
     flip_inputs(0, 1)
     flip_inputs(1, 1)
-    xt_copy = local(xt, xt_hbm)
     stage_e(0)
     stage_e(1)
     stage_f(0)
@@ -502,50 +493,32 @@
     for i in range(4 * SPLIT):
         arrived(pg.at[i * SUB : i * SUB + SUB], pg_r + i, away)
 
-    pg_copy = local(pg, pg_hbm)
+    pg_out[...] = pg[...]
     arrived(bs, mate_bias, away)
-    bias_copy = local(bs.at[0:1], bias_hbm)
+    bias_out[...] = bs[0:1, :]
     arrived(recs.at[:, pl.ds(mul(1 - k, 1024), 1024)], mate_rec)
-    rec_copy = local(recs, rec_hbm)
+    rec_out[...] = recs[...]
     for si, like, cond in sent:
         copy = rc_(like, like, si, 0, mate)
         if cond is None:
             copy.wait_send()
         else:
             pl.when(cond)(copy.wait_send)
-    dec_store(2).wait()
-    dec_store(3).wait()
-    for copy in (xt_copy, pg_copy, bias_copy, rec_copy):
-        copy.wait()
     assert (snum.count, rnum.count, lnum.count) == COUNTS, (snum.count, rnum.count, lnum.count)
 
 
-def outputs(rec_in, bias_in, pg_hbm, xt_hbm, dec_in, rec, enc, bias, dec, recv, biasv, pg, xt, encv, decv, sem):
-    def part(i):
-        return pl.ds(i * 256, 256)
-
-    loads = [pltpu.make_async_copy(pg_hbm, pg, sem.at[0]), pltpu.make_async_copy(xt_hbm, xt, sem.at[1])]
-    dec_loads = [pltpu.make_async_copy(dec_in.at[part(i)], decv.at[part(i)], sem.at[2 + i]) for i in range(4)]
-    dec_stores = [pltpu.make_async_copy(decv.at[part(i)], dec.at[part(i)], sem.at[6 + i]) for i in range(4)]
-    enc_store = pltpu.make_async_copy(encv, enc, sem.at[10])
-    small_loads = [pltpu.make_async_copy(rec_in, recv, sem.at[11]), pltpu.make_async_copy(bias_in, biasv, sem.at[12])]
-    small_stores = [pltpu.make_async_copy(recv, rec, sem.at[13]), pltpu.make_async_copy(biasv, bias, sem.at[14])]
-    for copy in loads + dec_loads + small_loads:
+def outputs(rec_in, bias_in, pg, xt, dec_in, rec, enc, bias, dec, encv, sem):
+    copies = [
+        pltpu.make_async_copy(dec_in, dec, sem.at[0]),
+        pltpu.make_async_copy(rec_in, rec, sem.at[1]),
+        pltpu.make_async_copy(bias_in, bias, sem.at[2]),
+        pltpu.make_async_copy(encv, enc, sem.at[3]),
+    ]
+    for copy in copies[:3]:
         copy.start()
-    for copy in loads:
-        copy.wait()
-    for i in range(2):
-        dec_loads[i].wait()
-        dec_stores[i].start()
     encv[...] = jnp.dot(xt[...], pg[...], preferred_element_type=F32).astype(BF)
-    enc_store.start()
-    for i in range(2, 4):
-        dec_loads[i].wait()
-        dec_stores[i].start()
-    for load, store in zip(small_loads, small_stores):
-        load.wait()
-        store.start()
-    for copy in dec_stores + small_stores + [enc_store]:
+    copies[3].start()
+    for copy in copies:
         copy.wait()
 
 
@@ -555,7 +528,6 @@
         pltpu.VMEM((16, 2048), BF),
         pltpu.VMEM((1, 256), F32),
         pltpu.VMEM((2, 2, 2, 2, 2, 16, 2048), BF),
-        pltpu.VMEM((2048, 512), BF),
         pltpu.VMEM((2048, 256), BF),
         pltpu.VMEM((1024, 2048), BF),
         pltpu.VMEM((2, 128, 256), BF),
@@ -582,23 +554,22 @@
         pltpu.VMEM((512, 256), BF),
         pltpu.VMEM((8, 256), F32),
         pltpu.VMEM((16, 2048), BF),
-        pltpu.VMEM((2, 1024, 512), BF),
         *[pltpu.SemaphoreType.DMA((n,)) for n in COUNTS],
     ]
     rec, bias, pg, xt, dec = pl.pallas_call(
         kernel,
         out_shape=(
-            jax.ShapeDtypeStruct((16, 2048), BF),
-            jax.ShapeDtypeStruct((1, 256), F32),
-            jax.ShapeDtypeStruct((512, 256), BF),
-            jax.ShapeDtypeStruct((2048, 512), BF),
-            jax.ShapeDtypeStruct((1024, 2048), BF),
+            pltpu.VMEM((16, 2048), BF),
+            pltpu.VMEM((1, 256), F32),
+            pltpu.VMEM((512, 256), BF),
+            pltpu.VMEM((2048, 512), BF),
+            pltpu.VMEM((1024, 2048), BF),
         ),
         in_specs=[hbm] * 5,
-        out_specs=[hbm] * 5,
+        out_specs=[vm] * 5,
         scratch_shapes=scratch,
         compiler_params=pltpu.CompilerParams(
-            collective_id=0, has_side_effects=True, vmem_limit_bytes=56 * 1024 * 1024
+            collective_id=0, has_side_effects=True, vmem_limit_bytes=48 * 1024 * 1024
         ),
         name="transcoder_step",
     )(
@@ -622,18 +593,10 @@
             jax.ShapeDtypeStruct((1, 256), F32),
             jax.ShapeDtypeStruct((1024, 2048), BF),
         ),
-        in_specs=[hbm] * 5,
+        in_specs=[vm] * 5,
         out_specs=[hbm] * 4,
-        scratch_shapes=[
-            pltpu.VMEM((16, 2048), BF),
-            pltpu.VMEM((1, 256), F32),
-            pltpu.VMEM((512, 256), BF),
-            pltpu.VMEM((2048, 512), BF),
-            pltpu.VMEM((2048, 256), BF),
-            pltpu.VMEM((1024, 2048), BF),
-            pltpu.SemaphoreType.DMA((15,)),
-        ],
-        compiler_params=pltpu.CompilerParams(vmem_limit_bytes=56 * 1024 * 1024),
+        scratch_shapes=[pltpu.VMEM((2048, 256), BF), pltpu.SemaphoreType.DMA((4,))],
+        compiler_params=pltpu.CompilerParams(vmem_limit_bytes=16 * 1024 * 1024),
         name="write_outputs",
     )(rec, bias, pg, xt, dec)
     return rec[None], enc[None], bias, dec.reshape(1, 4, 1, 256, 2048)

time: 76.5 us -> 73.5 us (0.961)
  Pallas kernels: 75.2 us -> 71.9 us
    pallas_call x1, Pallas kernels: 4.77 us -> 2.43 us  [shards(): pl.pallas_call(outputs, out_shape=(jax.ShapeDtypeStruct((16, 2048), BF),...]
    pallas_call x1, Pallas kernels: 70.4 us -> 69.5 us  [kernel1(): pl.pallas_call(kernel, out_shape=(pltpu.VMEM((16, 2048), BF), pltpu.VMEM(...]
where the time goes in v4:
time: 73.5 us; the launch traced here: 72.5 us
  Pallas kernels  71.9 us (98%)
    pallas_call x1, Pallas kernels, kernel1(): pl.pallas_call(kernel, out_shape=(pltpu.VMEM((16, 2048), BF), pltpu.VMEM(...  69.5 us
    pallas_call x1, Pallas kernels, shards(): pl.pallas_call(outputs, out_shape=(jax.ShapeDtypeStruct((16, 2048), BF),...  2.43 us

profile of v4, /device:TPU:8, one launch (start us, length us, event | category | flops | bytes accessed | tf_op | source)
XLA Modules:
  0.0 72.5 jit_solution(5171350982446778349)
XLA Ops:
  0.6 69.5 %transcoder_step.1 = (bf16[16,2048]{1,0:T(8,128)(2,1)S(1)}, f32[1,256]{1,0:T(1,128)S(1)}, bf16[512,256]{1,0:T(8,128)(2,1)S(1)}, bf16[2048,512]{1,0:T(8,128)(2,1)S(1)}, bf16[1024,2048]{1,0:T(8,128)(2,1)S(1)}) custom-call(bf16[2,2,2,2,16,2048]{5,4,3,2,1,0:T(8,128)(2,1)} %bitcast.10, bf16[16,2048]{1,0:T(8,128)(2,1)} %bitcast.12, bf16[2048,256]{1,0:T(8,128)(2,1)} %bitcast.11, ...), custom_call_target="tpu_custom_call" | custom-call | tf_op jit(solution)/shard_map/transcoder_step/pallas_call | solution.py:559
  70.1 2.4 %write_outputs.1 = (bf16[16,2048]{1,0:T(8,128)(2,1)}, bf16[2048,256]{1,0:T(8,128)(2,1)}, f32[1,256]{1,0:T(1,128)}, bf16[1024,2048]{1,0:T(8,128)(2,1)}) custom-call(bf16[16,2048]{1,0:T(8,128)(2,1)S(1)} %get-tuple-element.13.rec_in, f32[1,256]{1,0:T(1,128)S(1)} %get-tuple-element.14.bias_in, bf16[512,256]{1,0:T(8,128)(2,1)S(1)} %get-tuple-element.15.pg, ...), custom_call_target="tpu_custom_call" | custom-call | tf_op jit(solution)/shard_map/write_outputs/pallas_call | solution.py:588

commit v5 on v4

--- a/solution.py
+++ b/solution.py
@@ -8,7 +8,7 @@
 MESH = pl.DeviceIdType.MESH
 SPLIT = 2
 SUB = 128 // SPLIT
-COUNTS = (45, 113, 6)
+COUNTS = (46, 114, 6)
 BF = jnp.bfloat16
 F32 = jnp.float32
 
@@ -134,7 +134,7 @@
                 latb[m] = jnp.zeros((512, 256), BF)
 
     lat_r = rnum.take(16 * SPLIT)
-    mate_x, core_x, mate_t, mate_rec, mate_bias = (rnum.take() for _ in range(5))
+    mate_x, core_x, mate_t, mate_rec, mate_bias, line_x = (rnum.take() for _ in range(6))
     pg_r = rnum.take(4 * SPLIT)
     gr_r = rnum.take(20 * SPLIT)
 
@@ -210,7 +210,15 @@
                 at = 8 + (k * 2 + yh) * 2 + hh
                 send(t_ref.at[:, hh * 1024 + 512 : hh * 1024 + 1024], tg.at[at], si, mate_t, dev(dy=d))
         send(t_ref.at[:, there], slot, si, mate_t, mate)
-        send(xp.at[c, k], xp.at[c, k], group(xp.at[c, k]), mate_x, mate)
+        part = xp.at[c, k, x // 2, x % 2]
+        send(part, part, group(part), mate_x, mate)
+
+    def spread_inputs():
+        part = xp.at[c, 1 - k, x // 2, x % 2]
+        arrived(part, mate_x)
+        si = group(rx.at[0])
+        for d in (1, 2, 3):
+            send(part, part, si, line_x, dev(dx=d))
 
     def lat_hop(q, far):
         conds = []
@@ -447,6 +455,7 @@
     flip_inputs(0, 0)
     lat_hop(0, 2)
     lat_hop(1, 2)
+    spread_inputs()
     flip_inputs(1, 0)
     lat_hop(0, 3)
     lat_hop(1, 3)
@@ -461,7 +470,7 @@
     flip_latents(0)
     stage_a(1)
     flip_latents(1)
-    arrived(xp.at[c, 1 - k], mate_x)
+    arrived(rx.at[0], line_x)
     send(xp.at[c, 1 - k], xp.at[c, 1 - k], group(xp.at[c, 1 - k]), core_x, dev(flip=1))
     stage_b(0)
     stage_b(1)

time: 73.5 us -> 73.9 us (level)
  Pallas kernels: 71.9 us -> 72.9 us
    pallas_call x1, Pallas kernels: 69.5 us -> 70.5 us  [kernel1(): pl.pallas_call(kernel, out_shape=(pltpu.VMEM((16, 2048), BF), pltpu.VMEM(...]
where the time goes in v5:
time: 73.9 us; the launch traced here: 73.6 us
  Pallas kernels  72.9 us (99%)
    pallas_call x1, Pallas kernels, kernel1(): pl.pallas_call(kernel, out_shape=(pltpu.VMEM((16, 2048), BF), pltpu.VMEM(...  70.5 us
    pallas_call x1, Pallas kernels, shards(): pl.pallas_call(outputs, out_shape=(jax.ShapeDtypeStruct((16, 2048), BF),...  2.43 us

profile of v5, /device:TPU:8, one launch (start us, length us, event | category | flops | bytes accessed | tf_op | source)
XLA Modules:
  0.0 73.6 jit_solution(17535318798966099749)
XLA Ops:
  0.6 70.5 %transcoder_step.1 = (bf16[16,2048]{1,0:T(8,128)(2,1)S(1)}, f32[1,256]{1,0:T(1,128)S(1)}, bf16[512,256]{1,0:T(8,128)(2,1)S(1)}, bf16[2048,512]{1,0:T(8,128)(2,1)S(1)}, bf16[1024,2048]{1,0:T(8,128)(2,1)S(1)}) custom-call(bf16[2,2,2,2,16,2048]{5,4,3,2,1,0:T(8,128)(2,1)} %bitcast.10, bf16[16,2048]{1,0:T(8,128)(2,1)} %bitcast.12, bf16[2048,256]{1,0:T(8,128)(2,1)} %bitcast.11, ...), custom_call_target="tpu_custom_call" | custom-call | tf_op jit(solution)/shard_map/transcoder_step/pallas_call | solution.py:568
  71.2 2.4 %write_outputs.1 = (bf16[16,2048]{1,0:T(8,128)(2,1)}, bf16[2048,256]{1,0:T(8,128)(2,1)}, f32[1,256]{1,0:T(1,128)}, bf16[1024,2048]{1,0:T(8,128)(2,1)}) custom-call(bf16[16,2048]{1,0:T(8,128)(2,1)S(1)} %get-tuple-element.13.rec_in, f32[1,256]{1,0:T(1,128)S(1)} %get-tuple-element.14.bias_in, bf16[512,256]{1,0:T(8,128)(2,1)S(1)} %get-tuple-element.15.pg, ...), custom_call_target="tpu_custom_call" | custom-call | tf_op jit(solution)/shard_map/write_outputs/pallas_call | solution.py:597
